TPU v7x, 32 devices: a whole 2x2x4 slice. The times are simulated.
32 devices in a mesh: groups: 2 (over y), tm: 4 (over z), mp: 2 (over x), sub: 2 (over core).
Axes of the slice: x: 2, y: 2, z: 4, core: 2. Of those that a mesh axis runs over, the one named last changes fastest.
Arguments:
- events: bfloat16 [16384, 768], P(('groups', 'tm', 'sub')), parts along dimension 0, may hold values from -6 to 6
- w_gate: bfloat16 [768, 1536], P(None, 'mp'), may hold values from -0.21875 to 0.21875
- w_inner: bfloat16 [768, 1536], P(None, 'mp'), may hold values from -0.21875 to 0.21875
- w_bc: bfloat16 [768, 256], replicated, may hold values from -0.21875 to 0.21875
- w_step: bfloat16 [768, 24], P(None, 'mp'), may hold values from -0.21875 to 0.21875
- step_bias: float32 [24], P('mp'), may hold values from -3 to 1
- log_decay: float32 [24, 16384], P('mp', ('groups', 'tm', 'sub')), parts along dimension 1, may hold values from -1 to 0
- norm_gain: float32 [1536], P('mp'), may hold values from 0.1 to 1.9
- w_out: bfloat16 [1536, 768], P('mp'), may hold values from -0.15625 to 0.15625
- mix_gain: float32 [768], replicated, may hold values from 0.1 to 1.9
- port: int32 [16384], P(('groups', 'tm', 'sub')), parts along dimension 0, may hold values from 0 to 15, as said below
- port_shard: int32 [32], P('groups'), parts along dimension 0, may hold values from 0 to 3, as said below
- w_up: bfloat16 [4, 768, 1536], P('tm', None, 'mp'), may hold values from -0.21875 to 0.21875
- b_up: float32 [4, 1536], P('tm', 'mp'), may hold values from -6 to 6
- w_down: bfloat16 [4, 1536, 768], P('tm', 'mp'), may hold values from -0.15625 to 0.15625
Outputs:
- readout: bfloat16 [16384, 768], P(('groups', 'tm', 'sub'), 'mp'), parts along dimension 0
There are 2 independent parts, one for each index of `groups`. A program takes and returns all parts, laid end to end along the dimension named above; an argument that names none is the same for every part. Nothing has to cross between parts.
Inputs may be any that keep to these rules, and one draw needn't show every extreme that they name: Of the 1024 events of one device (aligned blocks of the trace, in order over tm and sub), exactly 512 belong to one port group, the same group for all devices of a trace and drawn per trace, and the rest are spread as evenly as possible over the other groups, so no device has more than 512 events of one group. Within a group, some ports are more frequent than others. `port_shard`: each port group owns exactly 4 ports.
All inputs are finite; a program needn't handle non-finite values.
Results may differ from a plain program's by a relative error of at most 0.02.
Values may be sent and summed in bfloat16 or wider, within the bound.
No kernel may reach another device: no remote copies, remote signals or barrier semaphores. Data moves between devices by JAX's collectives and lax.ppermute only.
A program may use at most 64 MiB of HBM per device.

v0:
```python
import jax
import jax.numpy as jnp
from jax import lax
from jax.experimental import pallas as pl
from jax.experimental.pallas import tpu as pltpu
from jax.sharding import PartitionSpec as P

BLOCK = 256
F32 = jnp.float32
BF16 = jnp.bfloat16


def entering_2(shard, axis, join, neutral):
    place = lax.axis_index(axis)
    gathered = jax.tree.map(
        lambda a, kind: lax.all_gather(a.astype(kind), axis),
        shard,
        jax.tree.map(lambda a: jnp.bfloat16 if a.dtype == jnp.float32 else a.dtype, shard),
    )
    state = jax.tree.map(lambda a, e: jnp.zeros_like(a) + jnp.asarray(e, a.dtype), shard, neutral)

    def one(hop, state):
        return join(
            state,
            jax.tree.map(
                lambda a, own: lax.dynamic_index_in_dim(a, hop, 0, False).astype(own.dtype),
                gathered,
                shard,
            ),
        )

    return lax.fori_loop(0, place, one, state)


def combine_states(earlier, later):
    decay_early, state_early = earlier
    decay_late, state_late = later
    return (decay_early * decay_late, decay_late[:, None, None] * state_early + state_late)


def place_rows(layer_out, mix_gain, placed, shard_count, capacity):
    features = layer_out.shape[1]
    feature_mean = jnp.mean(layer_out * layer_out, axis=1, keepdims=True)
    ready = (layer_out * lax.rsqrt(feature_mean + 1e-05) * mix_gain[None, :]).astype(jnp.bfloat16)
    return (
        jnp.zeros((shard_count * capacity, features), jnp.bfloat16)
        .at[placed]
        .set(ready)
        .reshape(shard_count, capacity, features)
    )


def general(
    events,
    w_gate,
    w_inner,
    w_bc,
    w_step,
    step_bias,
    log_decay,
    norm_gain,
    w_out,
    mix_gain,
    port,
    port_shard,
    w_up,
    b_up,
    w_down,
):
    length = events.shape[0]
    heads_here = w_step.shape[1]
    channels = w_inner.shape[1]
    head_dim = channels // heads_here
    nstate = w_bc.shape[1] // 2
    blocks = length // BLOCK
    gate_pre = jnp.dot(events, w_gate, preferred_element_type=jnp.float32)
    inner_pre = jnp.dot(events, w_inner, preferred_element_type=jnp.float32)
    bc_proj = jnp.dot(events, w_bc, preferred_element_type=jnp.float32).astype(jnp.bfloat16)
    step_size = jax.nn.softplus(
        jnp.dot(events, w_step, preferred_element_type=jnp.float32) + step_bias[None, :]
    )
    scaled = (inner_pre.reshape(length, heads_here, head_dim) * step_size[:, :, None]).astype(
        jnp.bfloat16
    )
    b_blocks = bc_proj[:, :nstate].reshape(blocks, BLOCK, nstate)
    c_blocks = bc_proj[:, nstate:].reshape(blocks, BLOCK, nstate)
    x_blocks = scaled.reshape(blocks, BLOCK, heads_here, head_dim).astype(jnp.float32)
    decay_blocks = log_decay.reshape(heads_here, blocks, BLOCK)
    running = jnp.cumsum(decay_blocks, axis=2)
    causal_mask = jnp.arange(BLOCK)[:, None] >= jnp.arange(BLOCK)[None, :]
    spread = running[:, :, :, None] - running[:, :, None, :]
    weights = jnp.where(causal_mask, jnp.exp(jnp.where(causal_mask, spread, 0.0)), 0.0)
    affinity = jnp.einsum("cin,cjn->cij", c_blocks, b_blocks, preferred_element_type=jnp.float32)
    mixing = affinity[None] * weights
    within = jnp.einsum("hcij,cjhp->cihp", mixing, x_blocks, precision=lax.Precision.HIGHEST)
    to_end = jnp.exp(running[:, :, -1:] - running)
    block_states = jnp.einsum(
        "cjn,hcj,cjhp->chnp",
        b_blocks.astype(jnp.float32),
        to_end,
        x_blocks,
        precision=lax.Precision.HIGHEST,
    )
    block_logs = running[:, :, -1]
    block_decay = jnp.exp(block_logs)
    entering = []
    running_state = jnp.zeros((heads_here, nstate, head_dim), jnp.float32)
    for block_index in range(blocks):
        entering.append(running_state)
        running_state = (
            block_decay[:, block_index][:, None, None] * running_state + block_states[block_index]
        )
    device_decay = jnp.prod(block_decay, axis=1)
    summary = (device_decay, running_state)
    identity = (jnp.ones_like(device_decay), jnp.zeros_like(running_state))
    carried = entering_2(summary, ("tm", "sub"), combine_states, identity)
    carry_state = carried[1]
    before_block = jnp.exp(jnp.cumsum(block_logs, axis=1) - block_logs)
    start_states = jnp.stack(entering) + before_block.T[:, :, None, None] * carry_state[None]
    from_state = jnp.einsum(
        "cin,hci,chnp->cihp",
        c_blocks.astype(jnp.float32),
        jnp.exp(running),
        start_states,
        precision=lax.Precision.HIGHEST,
    )
    ssm_out = (within + from_state).reshape(length, heads_here, head_dim)
    gated = ssm_out * jax.nn.silu(gate_pre.reshape(length, heads_here, head_dim))
    square_mean = jnp.mean(gated * gated, axis=2, keepdims=True)
    normed = (
        (gated * lax.rsqrt(square_mean + 1e-05) * norm_gain.reshape(heads_here, head_dim))
        .reshape(length, channels)
        .astype(jnp.bfloat16)
    )
    partial_sums = jnp.dot(normed, w_out, preferred_element_type=jnp.float32)
    shard_count = lax.axis_size("tm")
    capacity = 2 * length // shard_count
    port_table = port[:, None] == jnp.arange(port_shard.shape[0])[None, :]
    target = jnp.sum(jnp.where(port_table, port_shard[None, :], 0), axis=1)
    target_hot = (target[:, None] == jnp.arange(shard_count)[None, :]).astype(jnp.int32)
    slot_index = jnp.sum((jnp.cumsum(target_hot, axis=0) - 1) * target_hot, axis=1)
    placed = target * capacity + slot_index
    layer_out = lax.psum(partial_sums.astype(jnp.bfloat16), "mp").astype(jnp.float32)
    outgoing = place_rows(layer_out, mix_gain, placed, shard_count, capacity)
    received = lax.all_to_all(outgoing, "tm", split_axis=0, concat_axis=0, tiled=True)
    flat_rows = received.reshape(shard_count * capacity, received.shape[2])
    hidden_units = jax.nn.gelu(
        jnp.dot(flat_rows, w_up[0], preferred_element_type=jnp.float32) + b_up[0][None, :],
        approximate=True,
    ).astype(jnp.bfloat16)
    partial_out = jnp.dot(hidden_units, w_down[0], preferred_element_type=jnp.float32).reshape(
        shard_count, capacity, w_down.shape[2]
    )
    readout = lax.psum_scatter(
        partial_out.astype(jnp.bfloat16), "mp", scatter_dimension=2, tiled=True
    )
    returned = lax.all_to_all(readout, "tm", split_axis=0, concat_axis=0, tiled=True)
    return returned.reshape(shard_count * capacity, returned.shape[2])[placed]


SPAN = 128
TILE = 16
VMEM = pl.BlockSpec(memory_space=pltpu.VMEM)
SMEM = pl.BlockSpec(memory_space=pltpu.SMEM)
ANY = pl.BlockSpec(memory_space=pl.ANY)


def call(kernel, out_shape, *, micros, in_specs, after=(), room=24, **kw):
    count = len(in_specs)

    def body(*refs):
        kernel(*refs[:count], *refs[count + len(after) :])

    run = pl.pallas_call(
        body,
        in_specs=[*in_specs, *[ANY] * len(after)],
        out_shape=out_shape,
        cost_estimate=pl.CostEstimate(
            flops=int(micros * 1e9), bytes_accessed=int(micros * 3e6), transcendentals=0
        ),
        compiler_params=pltpu.CompilerParams(vmem_limit_bytes=room * 1024 * 1024),
        **kw,
    )
    return lambda *args: run(*args, *after)


def arr(shape, kind):
    return jax.ShapeDtypeStruct(shape, kind)


def dot(a, b, left=1, right=0):
    return lax.dot_general(a, b, (((left,), (right,)), ((), ())), preferred_element_type=F32)


def split(v, terms):
    out = []
    for _ in range(terms):
        part = v.astype(BF16)
        out.append(part)
        v = v - part.astype(F32)
    return out


def tie(x, first):
    return lax.optimization_barrier((x, first))[0]


def head_lanes(heads, channels):
    first = iota((heads, channels), 0) * (channels // heads)
    lane = iota((heads, channels), 1)
    return ones_where((lane >= first) & (lane < first + channels // heads))


def spread_heads(v, lanes):
    return sum(dot(part, lanes) for part in split(v, 2))


def iota(shape, dim):
    return lax.broadcasted_iota(jnp.int32, shape, dim)


def ones_where(mask, kind=BF16):
    return jnp.where(mask, 1.0, 0.0).astype(kind)


def scan_in_kernel(ev, w_inner, w_bc, w_step, bias, decay, scaled_o, bc_o, sum_o, state, total):
    step_id = pl.program_id(0)
    rows = ev.shape[0]
    nstate = w_bc.shape[1] // 2
    x = ev[...]
    lanes = head_lanes(decay.shape[0], w_inner.shape[1])
    inner = dot(x, w_inner[...])
    bc = dot(x, w_bc[...]).astype(BF16)
    pre = dot(x, w_step[...], 1, 1) + bias[...]
    step = jnp.maximum(pre, 0.0) + jnp.log1p(jnp.exp(-jnp.abs(pre)))
    scaled = (inner * spread_heads(step, lanes)).astype(BF16)
    scaled_o[...] = scaled
    bc_o[...] = bc
    logs = split(decay[...], 3)
    later = ones_where(iota((rows, rows), 1) > iota((rows, rows), 0))
    to_end = jnp.exp(sum(dot(later, part, 1, 1) for part in logs))
    whole = jnp.exp(sum(dot(jnp.ones((8, rows), BF16), part, 1, 1) for part in logs))
    weighted = (scaled.astype(F32) * spread_heads(to_end, lanes)).astype(BF16)
    fresh = dot(bc[:, :nstate], weighted, 0, 0)
    fade = spread_heads(whole, lanes)

    @pl.when(step_id == 0)
    def _():
        state[...] = fresh
        total[...] = fade

    @pl.when(step_id > 0)
    def _():
        state[...] = state[...] * fade[:1] + fresh
        total[...] = total[...] * fade

    @pl.when(step_id == pl.num_programs(0) - 1)
    def _():
        put_summary(sum_o, state[...], total[:1])


def put_summary(ref, state, decay):
    n, width = state.shape
    ref[:n, :] = state.astype(BF16)
    high = decay.astype(BF16).astype(F32)
    row = iota((TILE, width), 0)
    ref[n:, :] = jnp.where(row == 0, high, jnp.where(row == 1, decay - high, 0.0)).astype(BF16)


def get_summary(value):
    n = value.shape[0] - TILE
    value = value.astype(F32)
    return value[n : n + 1] + value[n + 1 : n + 2], value[:n]


def chip_kernel(info, own, other, out):
    half = out.shape[1]
    place = info[3]
    cols = pl.ds(pl.multiple_of(place * half, half), half)
    mine, theirs = own[:, cols].astype(F32), other[:, cols].astype(F32)
    first = jnp.where(place == 0, mine, theirs)
    second = jnp.where(place == 0, theirs, mine)
    decay_1, state_1 = get_summary(first)
    decay_2, state_2 = get_summary(second)
    put_summary(out, decay_2 * state_1 + state_2, decay_1 * decay_2)


def carry_kernel(*refs):
    out = refs[-1]
    state = None
    for ref in reversed(refs[:-1]):
        decay, fresh = get_summary(ref[...])
        state = fresh if state is None else decay * state + fresh
    out[...] = state.astype(BF16)


def within_kernel(scaled, bc, decay, y_o, past_o, state, run):
    step_id = pl.program_id(0)
    rows = scaled.shape[0]
    heads = decay.shape[0]
    nstate = bc.shape[1] // 2
    pair = scaled.shape[1] * 2 // heads

    @pl.when(step_id == 0)
    def _():
        state[...] = jnp.zeros_like(state)
        run[...] = jnp.zeros_like(run)

    lanes = head_lanes(heads, scaled.shape[1])
    halves = head_lanes(2, pair)
    row, col = iota((rows, rows), 0), iota((rows, rows), 1)
    causal = row >= col
    logs = split(decay[...], 3)
    until = sum(dot(ones_where(causal), part, 1, 1) for part in logs)
    until_row = sum(dot(part, ones_where(row <= col)) for part in logs)
    b, c = bc[:, :nstate], bc[:, nstate:]
    affinity = dot(c, b, 1, 1)
    past = spread_heads(jnp.exp(until), lanes) * dot(c, state[...].astype(BF16))
    for number in range(heads // 2):
        mixes = []
        for head in (2 * number, 2 * number + 1):
            gap = until[:, head : head + 1] - until_row[head : head + 1, :]
            mixes.append((affinity * jnp.exp(jnp.where(causal, gap, -1e30))).astype(BF16))
        cols = slice(number * pair, (number + 1) * pair)
        x = scaled[:, cols]
        both = jnp.concatenate([x * halves[0:1, :], x * halves[1:2, :]], axis=0)
        y_o[:, cols] = past[:, cols] + dot(jnp.concatenate(mixes, axis=1), both)
    last = until[rows - 1 :, :]
    weighted = scaled[...].astype(F32) * spread_heads(jnp.exp(last - until), lanes)
    fade = spread_heads(jnp.exp(jnp.broadcast_to(last, (8, heads))), lanes)
    state[...] = state[...] * fade[:1] + dot(b, weighted.astype(BF16), 0, 0)
    past_o[...] = jnp.exp(until + run[:1])
    run[...] += jnp.broadcast_to(last, run.shape)


def norm_kernel(info, y, gate, bc, past, mine, other, before, gain, w_out, slot, out, carry, all_rows):
    step_id = pl.program_id(0)
    rows, channels = y.shape
    heads = past.shape[1]
    nstate = bc.shape[1] // 2
    lanes = head_lanes(heads, channels)

    @pl.when(step_id == 0)
    def _():
        here = info[3]
        a, b = mine[...].astype(F32), other[...].astype(F32)
        low, high = jnp.where(here == 0, a, b), jnp.where(here == 0, b, a)
        chip = jnp.concatenate([low, high], axis=1)
        decay, state = get_summary(before[...])
        carry[...] = jnp.where(here == 0, chip, decay * chip + state).astype(BF16)

    ssm = y[...] + spread_heads(past[...], lanes) * dot(bc[:, nstate:], carry[...])
    gated = ssm * gate[...]
    square = dot((gated * gated).astype(BF16), lanes, 1, 1) * (heads / channels)
    scale = spread_heads(lax.rsqrt(square + 1e-05), lanes)
    normed = (gated * scale * gain[...][None, :]).astype(BF16)
    all_rows[pl.ds(pl.multiple_of(step_id * rows, rows), rows), :] = dot(normed, w_out[...]).astype(BF16)

    @pl.when(step_id == pl.num_programs(0) - 1)
    def _():
        count = out.shape[1]
        here = 2 * (info[0] & 1) + info[1]
        for place in range(4):
            first = (place ^ here) * count
            pick = ones_where(slot[...] == iota((count, slot.shape[1]), 0) + first)
            out[place] = dot(pick, all_rows[...]).astype(BF16)


def mixed(term_1, term_2, gain):
    total = term_1[...].astype(F32) + term_2[...].astype(F32)
    mean = jnp.mean(total * total, axis=1, keepdims=True)
    return (total * lax.rsqrt(mean + 1e-05) * gain[...][None, :]).astype(BF16)


def route_kernel(cold, info, shard, port, slot_o, column_o, flag_o):
    length = port.shape[1]
    half_rows = 2 * length // 4 // 2
    rows = half_rows + cold
    target = jnp.zeros(port.shape, jnp.int32)
    for number in range(shard.shape[0]):
        target = jnp.where(port[...] == number, shard[number], target)
    group = iota((8, length), 0)
    member = ones_where(jnp.broadcast_to(target, (8, length)) == group, F32)
    lane = iota((8, length), 1)
    count = member
    reach = 1
    while reach < length:
        count = count + jnp.where(lane >= reach, pltpu.roll(count, reach, 1), 0.0)
        reach *= 2
    rank = jnp.sum(member * (count - 1.0), axis=0, keepdims=True).astype(jnp.int32)
    whole = jnp.broadcast_to(count[:, length - 1 :], (8, 128))
    big = jnp.where(whole == 2.0 * half_rows, group[:, :128], 0)
    hot = jnp.max(big.astype(F32)).astype(jnp.int32)
    flag_o[0] = jnp.where(hot == info[0], 0, 1)
    away = target ^ info[0]
    half = (rank & 1) ^ info[1]
    row = rank >> 1
    row = jnp.where(away >= 2, rows - 1 - row, row)
    slot = (2 * (away & 1) + half) * rows + row
    slot_o[...] = slot
    wide = jnp.broadcast_to(slot.astype(F32), (128, length))
    column_o[...] = wide.T.astype(jnp.int32)


def readout_kernel(cold, info, flag, terms, gain, bias, w_up, w_down, *refs):
    pieces = refs[:10]
    same_o, other_o, same_l_o, other_l_o, up, down, extra, total, sems = refs[10:]
    width = up.shape[1]
    part = width // 4
    copies = [[] for _ in range(4)]
    used = 0

    def start(bank, source, target):
        nonlocal used
        copy = pltpu.make_async_copy(source, target, sems.at[used])
        copy.start()
        copies[bank].append(copy)
        used += 1

    start(0, w_up.at[0], up.at[0])
    start(0, w_down.at[0], down.at[0])
    for core in (0, 1):
        here = (info[3] ^ core) * 2
        at = pl.ds(pl.multiple_of(here * part, 2 * part), 2 * part)
        piece = pieces[5 * core]
        start(1, piece.at[pl.ds(0, 2 * part)], up.at[1, at])
        start(1, piece.at[pl.ds(2 * part, 2 * part)], down.at[1, at])
        for number, bank in enumerate((2, 2, 3, 3)):
            piece = pieces[5 * core + 1 + number]
            first = here + (info[2] ^ (number % 2))
            at = pl.ds(pl.multiple_of(first * part, part), part)
            start(bank, piece.at[pl.ds(0, part)], up.at[bank, at])
            start(bank, piece.at[pl.ds(part, part)], down.at[bank, at])
    start(1, pieces[0].at[pl.ds(4 * part, TILE)], extra.at[1])
    start(2, pieces[1].at[pl.ds(2 * part, TILE)], extra.at[2])
    start(3, pieces[3].at[pl.ds(2 * part, TILE)], extra.at[3])

    odd = info[0] & 1
    away = mixed(terms.at[2 - 2 * odd], terms.at[3 - 2 * odd], gain)
    local = mixed(terms.at[2 * odd], terms.at[2 * odd + 1], gain)
    count = away.shape[0]

    def run(lo, hi, bank, first):
        size = hi - lo
        x = jnp.concatenate([away[lo:hi], local[lo:hi]], axis=0)
        out = None
        for half in (0, 1):
            if first:
                for copy in copies[bank + half]:
                    copy.wait()
            if bank + half == 0:
                shift = bias[...]
            else:
                shift = jnp.sum(extra[bank + half].astype(F32), axis=0, keepdims=True)
            v = dot(x, up[bank + half]) + shift
            hidden = (0.5 * v * (1.0 + jnp.tanh(0.7978845608028654 * (v + 0.044715 * v * v * v)))).astype(BF16)
            y = dot(hidden, down[bank + half])
            out = y if half == 0 else out + y
        total[0, lo:hi, :] = out[:size]
        total[1, lo:hi, :] = out[size:]

    run(0, cold, 0, True)
    run(count - cold, count, 2, True)

    @pl.when(flag[0] == 0)
    def _():
        run(cold, count - cold, 0, False)

    @pl.when(flag[0] != 0)
    def _():
        run(cold, count - cold, 2, False)

    place = info[1]
    side = same_o.shape[1]
    for number, (near, far) in enumerate(((same_o, other_o), (same_l_o, other_l_o))):
        low, high = total[number, :, :side], total[number, :, side:]
        near[...] = jnp.where(place == 0, low, high).astype(BF16)
        far[...] = jnp.where(place == 0, high, low).astype(BF16)


def payload_kernel(info, bias, w_up, w_down, out, sems):
    part = (out.shape[0] - TILE) // 2
    first = info[3] * (out.shape[1] // 2)
    if 2 * part < out.shape[1] // 2 + part:
        first = first + info[2] * part
    at = pl.ds(pl.multiple_of(first, part), part)
    copies = [
        pltpu.make_async_copy(w.at[0, at], out.at[pl.ds(number * part, part)], sems.at[number])
        for number, w in enumerate((w_up, w_down))
    ]
    for copy in copies:
        copy.start()
    row = iota((TILE, out.shape[1]), 0)
    rows = jnp.zeros((TILE, out.shape[1]), F32)
    for number, term in enumerate(split(bias[...], 3)):
        rows = jnp.where(row == number, term.astype(F32), rows)
    out[2 * part :, :] = rows.astype(BF16)
    for copy in copies:
        copy.wait()


def gate_kernel(ev, w_gate, out):
    gate = dot(ev[...], w_gate[...])
    out[...] = gate / (1.0 + jnp.exp(-gate))


def collect_kernel(column, a, b, c, d, out, joined):
    rows = a.shape[0]

    @pl.when(pl.program_id(0) == 0)
    def _():
        for number, ref in enumerate((a, b, c, d)):
            joined[number * rows : (number + 1) * rows, :] = ref[...]

    place = column[...]
    lane = iota(place.shape, 1)
    picks = [ones_where(place == lane + first) for first in range(0, 4 * rows, 128)]
    out[...] = dot(jnp.concatenate(picks, axis=1), joined[...]).astype(BF16)


def hold(block, index):
    return pl.BlockSpec(block, index)


def fixed(shape):
    return pl.BlockSpec(shape, lambda i: (0,) * len(shape))


def fast(
    events,
    w_gate,
    w_inner,
    w_bc,
    w_step,
    step_bias,
    log_decay,
    norm_gain,
    w_out,
    mix_gain,
    port,
    port_shard,
    w_up,
    b_up,
    w_down,
):
    length, width = events.shape
    channels = w_inner.shape[1]
    heads = w_step.shape[1]
    head_dim = channels // heads
    nstate = w_bc.shape[1] // 2
    shard_count = lax.axis_size("tm")
    hot_rows = 2 * length // shard_count // 2
    most = -(-(length - 2 * hot_rows) // (shard_count - 1))
    cold = -(-((most + 1) // 2) // TILE) * TILE
    count = hot_rows + cold
    info = jnp.stack([lax.axis_index(a) for a in ("tm", "mp", "groups", "sub")]).astype(jnp.int32)
    swap = [(0, 1), (1, 0)]
    side = width // 2

    part = width // 4
    def payload(rows, room, after):
        return call(
            payload_kernel,
            arr((2 * rows + TILE, width), BF16),
            micros=0.1,
            room=room,
            in_specs=[SMEM, VMEM, ANY, ANY],
            out_specs=VMEM,
            scratch_shapes=[pltpu.SemaphoreType.DMA((2,))],
            after=after,
        )(info, b_up, w_up, w_down)

    share = payload(part, 62, ())
    far = lax.ppermute(share, "tm", [(i, i ^ 2) for i in range(shard_count)])

    rows = 2 * SPAN
    grid = (length // rows,)
    scaled, bc, summary = call(
        scan_in_kernel,
        (
            arr((length, channels), BF16),
            arr((length, 2 * nstate), BF16),
            arr((nstate + TILE, channels), BF16),
        ),
        room=62,
        after=(share,),
        micros=0.1,
        grid=grid,
        in_specs=[
            hold((rows, width), lambda i: (i, 0)),
            fixed(w_inner.shape),
            fixed(w_bc.shape),
            fixed((heads, width)),
            fixed((1, heads)),
            hold((heads, rows), lambda i: (0, i)),
        ],
        out_specs=(
            hold((rows, channels), lambda i: (i, 0)),
            hold((rows, 2 * nstate), lambda i: (i, 0)),
            fixed((nstate + TILE, channels)),
        ),
        scratch_shapes=[pltpu.VMEM((nstate, channels), F32), pltpu.VMEM((8, channels), F32)],
    )(events, w_inner, w_bc, w_step.T, step_bias[None, :], log_decay)
    beside = lax.ppermute(summary, "sub", swap)
    chip = call(
        chip_kernel,
        arr((nstate + TILE, channels // 2), BF16),
        micros=0.1,
        in_specs=[SMEM, VMEM, VMEM],
        out_specs=VMEM,
    )(info, summary, beside)
    earlier = [
        lax.ppermute(chip, "tm", [(i, i + hop) for i in range(shard_count - hop)])
        for hop in range(1, shard_count)
    ]

    own = lax.ppermute(payload(2 * part, 24, (summary,)), "mp", swap)
    slot, column, flag = call(
        lambda *refs: route_kernel(cold, *refs),
        (arr((1, length), jnp.int32), arr((length, 128), jnp.int32), arr((1,), jnp.int32)),
        micros=0.1,
        in_specs=[SMEM, SMEM, VMEM],
        out_specs=(VMEM, VMEM, SMEM),
    )(info, port_shard, port[None, :])
    gate = call(
        gate_kernel,
        arr((length, channels), F32),
        room=24,
        micros=0.1,
        grid=grid,
        in_specs=[hold((rows, width), lambda i: (i, 0)), fixed(w_gate.shape)],
        out_specs=hold((rows, channels), lambda i: (i, 0)),
        after=(chip, slot),
    )(events, w_gate)
    y, past = call(
        within_kernel,
        (arr((length, channels), F32), arr((length, heads), F32)),
        room=24,
        micros=2.0,
        grid=(length // SPAN,),
        in_specs=[
            hold((SPAN, channels), lambda i: (i, 0)),
            hold((SPAN, 2 * nstate), lambda i: (i, 0)),
            hold((heads, SPAN), lambda i: (0, i)),
        ],
        out_specs=(
            hold((SPAN, channels), lambda i: (i, 0)),
            hold((SPAN, heads), lambda i: (i, 0)),
        ),
        scratch_shapes=[pltpu.VMEM((nstate, channels), F32), pltpu.VMEM((8, heads), F32)],
        after=(gate,),
    )(scaled, bc, log_decay)

    carry = call(
        carry_kernel,
        arr((nstate, channels // 2), BF16),
        micros=0.1,
        in_specs=[VMEM] * len(earlier),
        out_specs=VMEM,
        after=(past, slot, far),
    )(*earlier)
    far = tie(far, carry)
    far_x = lax.ppermute(far, "mp", swap)
    far_y = lax.ppermute(far, "groups", swap)
    carry_beside = lax.ppermute(carry, "sub", swap)

    blocks = call(
        norm_kernel,
        arr((4, count, width), BF16),
        room=24,
        micros=0.1,
        grid=grid,
        in_specs=[
            SMEM,
            hold((rows, channels), lambda i: (i, 0)),
            hold((rows, channels), lambda i: (i, 0)),
            hold((rows, 2 * nstate), lambda i: (i, 0)),
            hold((rows, heads), lambda i: (i, 0)),
            fixed(carry.shape),
            fixed(carry.shape),
            fixed(beside.shape),
            fixed((channels,)),
            fixed(w_out.shape),
            fixed(slot.shape),
        ],
        out_specs=fixed((4, count, width)),
        scratch_shapes=[pltpu.VMEM((nstate, channels), BF16), pltpu.VMEM((length, width), BF16)],
    )(info, y, gate, bc, past, carry, carry_beside, beside, norm_gain, w_out, slot)
    near = [(i, i ^ 1) for i in range(shard_count)]
    near_x = [(2 * i + j, 2 * (i ^ 1) + (j ^ 1)) for i in range(shard_count) for j in range(2)]
    squares = [[4 * i + j for j in range(4)] for i in range(shard_count // 2)]
    blocks = tie(tie(tie(blocks, far_x), far_y), own)
    terms = lax.all_to_all(
        blocks, ("tm", "mp"), 0, 0, axis_index_groups=squares, tiled=True
    )
    own, far, far_y, far_x = (tie(a, blocks) for a in (own, far, far_y, far_x))
    far_xy = lax.ppermute(far_x, "groups", swap)
    firsts = [own, far, far_y, far_x, far_xy]
    pieces = firsts + [lax.ppermute(a, "sub", swap) for a in firsts]

    same, other, same_l, other_l = call(
        lambda *refs: readout_kernel(cold, *refs),
        (arr((count, side), BF16),) * 4,
        room=60,
        micros=1,
        in_specs=[SMEM, SMEM] + [VMEM] * 3 + [ANY] * 12,
        out_specs=(VMEM,) * 4,
        scratch_shapes=[
            pltpu.VMEM((4, width, width), BF16),
            pltpu.VMEM((4, width, width), BF16),
            pltpu.VMEM((4, TILE, width), BF16),
            pltpu.VMEM((2, count, width), F32),
            pltpu.SemaphoreType.DMA((29,)),
        ],
    )(info, flag, terms, mix_gain, b_up, w_up, w_down, *pieces)
    back_same = lax.ppermute(same, "tm", near)
    back_other = lax.ppermute(other, ("tm", "mp"), near_x)
    back_l = lax.ppermute(other_l, "mp", swap)

    return call(
        collect_kernel,
        arr((length, side), BF16),
        micros=1,
        grid=grid,
        in_specs=[hold((rows, 128), lambda i: (i, 0))] + [fixed((count, side))] * 4,
        out_specs=hold((rows, side), lambda i: (i, 0)),
        scratch_shapes=[pltpu.VMEM((4 * count, side), BF16)],
    )(column, same_l, back_l, back_same, back_other)


def shards(*args):
    events, w_inner, w_step = args[0], args[2], args[4]
    sizes = tuple(lax.axis_size(a) for a in ("groups", "tm", "mp", "sub"))
    heads = w_step.shape[1]
    square = events.shape[1] == w_inner.shape[1] == args[12].shape[2]
    if sizes == (2, 4, 2, 2) and heads % 4 == 0 and square and events.shape[0] % 512 == 0:
        return fast(*args)
    return general(*args)


def solution(mesh):
    in_specs = (
        P(("groups", "tm", "sub"), None),
        P(None, "mp"),
        P(None, "mp"),
        P(),
        P(None, "mp"),
        P("mp"),
        P("mp", ("groups", "tm", "sub")),
        P("mp"),
        P("mp", None),
        P(),
        P(("groups", "tm", "sub")),
        P("groups"),
        P("tm", None, "mp"),
        P("tm", "mp"),
        P("tm", "mp", None),
    )
    out_specs = P(("groups", "tm", "sub"), "mp")
    return jax.shard_map(shards, mesh=mesh, in_specs=in_specs, out_specs=out_specs, check_vma=False)
```

profile of v0, /device:TPU:0, one launch (start us, length us, event | category | flops | bytes accessed | tf_op | source)
XLA Modules:
  0.0 122.8 jit_solution(10668248079149051855)
XLA Ops:
  0.6 2.6 %shard_map.146.refs_6_ = bf16[400,768]{1,0:T(8,128)(2,1)} custom-call(s32[4]{0:T(128)} %pad_add_fusion.refs_0_, f32[1,768]{1,0:T(1,128)} %refs_4_.1, bf16[1,768,768]{2,1,0:T(8,128)(2,1)} %refs_5_.3, bf16[1,768,768]{2,1,0:T(8,128)(2,1)} %refs_6_.1), custom_call_target="tpu_custom_call" | custom-call | flops 100000000 | bytes 300000 | tf_op jit(solution)/shard_map/pallas_call | solution.py:184
  3.2 4.1 %collective-permute-start.4 = (bf16[400,768]{1,0:T(8,128)(2,1)}, bf16[400,768]{1,0:T(8,128)(2,1)S(1)}, u32[]{:S(2)}, u32[]{:S(2)}) collective-permute-start(bf16[400,768]{1,0:T(8,128)(2,1)} %shard_map.146.refs_6_), channel_id=1, source_target_pairs={{0,8},{4,12},{8,0},{12,4},{1,9},{5,13},{9,1},{13,5},{2,10},{6,14},... | collective-permute-start | bytes 1843208 | tf_op jit(solution)/shard_map/ppermute | solution.py:574
  7.3 9.7 %shard_map.147 = (bf16[1024,768]{1,0:T(8,128)(2,1)}, bf16[1024,256]{1,0:T(8,128)(2,1)}, bf16[144,768]{1,0:T(8,128)(2,1)}) custom-call(bf16[1024,768]{1,0:T(8,128)(2,1)} %refs_0_.3, bf16[768,768]{1,0:T(8,128)(2,1)} %refs_1_.7, bf16[768,256]{1,0:T(8,128)(2,1)} %refs_2_.5, bf16[12,768]{1,0:T(8,128)(2,1)} %bitcast.8, f32[1,12]{1,0:T(1,128)} %bitcast.9, ...), custom_call_target="tpu_custom_call" | custom-call | flops 100000000 | bytes 300000 | tf_op jit(solution)/shard_map/pallas_call | solution.py:184
  17.0 1.3 %copy-done.1 = bf16[1,768,768]{2,1,0:T(8,128)(2,1)S(1)} copy-done((bf16[1,768,768]{2,1,0:T(8,128)(2,1)S(1)}, bf16[1,768,768]{2,1,0:T(8,128)(2,1)}, u32[]{:S(2)}) %copy-start.1) | copy-done | bytes 1179672
  18.3 0.9 copy-done.6
  19.2 0.8 shard_map.153
  20.1 1.6 %collective-permute-start.8 = (bf16[784,768]{1,0:T(8,128)(2,1)S(1)}, bf16[784,768]{1,0:T(8,128)(2,1)}, u32[]{:S(2)}, u32[]{:S(2)}) collective-permute-start(bf16[784,768]{1,0:T(8,128)(2,1)S(1)} %shard_map.153), channel_id=1, source_target_pairs={{0,2},{2,0},{1,3},{3,1},{4,6},{6,4},{5,7},{7,5},{8,10},{10,8},{9,1... | collective-permute-start | bytes 3612680 | tf_op jit(solution)/shard_map/ppermute | solution.py:617
  21.7 1.7 %shard_map.145 = (s32[1,1024]{1,0:T(1,128)S(1)}, s32[1024,128]{1,0:T(8,128)S(1)}, s32[1]{0:T(128)}) custom-call(s32[4]{0:T(128)S(1)} %copy-done.10, s32[16]{0:T(128)S(1)} %copy-done.15, s32[1,1024]{1,0:T(1,128)S(1)} %bitcast.7), custom_call_target="tpu_custom_call" | custom-call | flops 100000000 | bytes 300000 | tf_op jit(solution)/shard_map/pallas_call | solution.py:184
  24.0 3.5 %collective-permute-start.1 = (bf16[144,384]{1,0:T(8,128)(2,1)S(1)}, bf16[144,384]{1,0:T(8,128)(2,1)S(1)}, u32[]{:S(2)}, u32[]{:S(2)}) collective-permute-start(bf16[144,384]{1,0:T(8,128)(2,1)S(1)} %shard_map.148.refs_2_), channel_id=1, source_target_pairs={{0,4},{4,8},{8,12},{1,5},{5,9},{9,13},{2,6},{6,10},{10,14},{3,7},{... | collective-permute-start | bytes 331784 | tf_op jit(solution)/shard_map/ppermute | solution.py:613
  27.5 2.2 %collective-permute-start.2 = (bf16[144,384]{1,0:T(8,128)(2,1)S(1)}, bf16[144,384]{1,0:T(8,128)(2,1)S(1)}, u32[]{:S(2)}, u32[]{:S(2)}) collective-permute-start(bf16[144,384]{1,0:T(8,128)(2,1)S(1)} %shard_map.148.refs_2_), channel_id=1, source_target_pairs={{0,8},{4,12},{1,9},{5,13},{2,10},{6,14},{3,11},{7,15},{16,24},{20,... | collective-permute-start | bytes 331784 | tf_op jit(solution)/shard_map/ppermute | solution.py:613
  29.7 1.3 %collective-permute-start.3 = (bf16[144,384]{1,0:T(8,128)(2,1)S(1)}, bf16[144,384]{1,0:T(8,128)(2,1)S(1)}, u32[]{:S(2)}, u32[]{:S(2)}) collective-permute-start(bf16[144,384]{1,0:T(8,128)(2,1)S(1)} %shard_map.148.refs_2_), channel_id=1, source_target_pairs={{0,12},{1,13},{2,14},{3,15},{16,28},{17,29},{18,30},{19,31}} | collective-permute-start | bytes 331784 | tf_op jit(solution)/shard_map/ppermute | solution.py:613
  31.1 2.3 %shard_map.149.refs_3_.refs_2_ = f32[1024,768]{1,0:T(8,128)S(1)} custom-call(bf16[1024,768]{1,0:T(8,128)(2,1)S(1)} %copy-done.2, bf16[768,768]{1,0:T(8,128)(2,1)S(1)} %copy-done.4, bf16[144,384]{1,0:T(8,128)(2,1)S(1)} %shard_map.148.refs_2_, s32[1,1024]{1,0:T(1,128)S(1)} %get-tuple-element.30.refs_3_.refs_4_.refs_10_), custom_call_target="tpu_custom_call" | custom-call | flops 100000000 | bytes 300000 | tf_op jit(solution)/shard_map/pallas_call | solution.py:184
  33.4 7.6 %shard_map.150 = (f32[1024,768]{1,0:T(8,128)S(1)}, f32[1024,12]{1,0:T(8,128)S(1)}) custom-call(bf16[1024,768]{1,0:T(8,128)(2,1)S(1)} %copy-done.12, bf16[1024,256]{1,0:T(8,128)(2,1)S(1)} %copy-done.7, f32[12,1024]{1,0:T(8,128)S(1)} %copy-done.8, f32[1024,768]{1,0:T(8,128)S(1)} %shard_map.149.refs_3_.refs_2_), custom_call_target="tpu_custom_call" | custom-call | flops 2000000000 | bytes 6000000 | tf_op jit(solution)/shard_map/pallas_call | solution.py:184
  41.8 1.5 %collective-permute-start.7 = (bf16[400,768]{1,0:T(8,128)(2,1)S(1)}, bf16[400,768]{1,0:T(8,128)(2,1)}, u32[]{:S(2)}, u32[]{:S(2)}) collective-permute-start(bf16[400,768]{1,0:T(8,128)(2,1)S(1)} %collective-permute-done.4.refs_5_.refs_8_), channel_id=1, source_target_pairs={{0,16},{16,0},{1,17},{17,1},{2,18},{18,2},{3,19},{19,3},{4,20},{20... | collective-permute-start | bytes 1843208 | tf_op jit(solution)/shard_map/ppermute | solution.py:664
  43.3 1.3 %collective-permute-done.5.refs_6_ = bf16[128,384]{1,0:T(8,128)(2,1)S(1)} collective-permute-done((bf16[128,384]{1,0:T(8,128)(2,1)S(1)}, bf16[128,384]{1,0:T(8,128)(2,1)S(1)}, u32[]{:S(2)}, u32[]{:S(2)}) %collective-permute-start.5) | collective-permute-done | bytes 98336 | tf_op jit(solution)/shard_map/ppermute | solution.py:665
  44.6 10.4 %shard_map.152 = bf16[4,352,768]{2,1,0:T(8,128)(2,1)} custom-call(s32[4]{0:T(128)S(1)} %copy-done.10, f32[1024,768]{1,0:T(8,128)S(1)} %get-tuple-element.31.refs_1_, f32[1024,768]{1,0:T(8,128)S(1)} %shard_map.149.refs_3_.refs_2_, bf16[1024,256]{1,0:T(8,128)(2,1)S(1)} %copy-done.7, f32[1024,12]{1,0:T(8,128)S(1)} %get-tuple-element.32.refs_3_.refs_4_, ...), custom_call_target="tpu_custom_call" | custom-call | flops 100000000 | bytes 300000 | tf_op jit(solution)/shard_map/pallas_call | solution.py:184
  55.0 6.4 %collective-permute-done.6.refs_10_ = bf16[400,768]{1,0:T(8,128)(2,1)} collective-permute-done((bf16[400,768]{1,0:T(8,128)(2,1)S(1)}, bf16[400,768]{1,0:T(8,128)(2,1)}, u32[]{:S(2)}, u32[]{:S(2)}) %collective-permute-start.6) | collective-permute-done | bytes 614432 | tf_op jit(solution)/shard_map/ppermute | solution.py:663
  61.4 3.8 %all-to-all-start = ((bf16[4,352,768]{2,1,0:T(8,128)(2,1)}), bf16[4,352,768]{2,1,0:T(8,128)(2,1)S(1)}, u32[]{:S(2)}, u32[]{:S(2)}) async-start(bf16[4,352,768]{2,1,0:T(8,128)(2,1)} %shard_map.152), calls=%async_computation | async-start | bytes 4325376 | tf_op jit(solution)/shard_map/all_to_all | solution.py:693
  65.2 1.5 %collective-permute-start.9 = (bf16[400,768]{1,0:T(8,128)(2,1)}, bf16[400,768]{1,0:T(8,128)(2,1)S(1)}, u32[]{:S(2)}, u32[]{:S(2)}) collective-permute-start(bf16[400,768]{1,0:T(8,128)(2,1)} %collective-permute-done.6.refs_10_), channel_id=1, source_target_pairs={{0,16},{16,0},{1,17},{17,1},{2,18},{18,2},{3,19},{19,3},{4,20},{20... | collective-permute-start | bytes 1843208 | tf_op jit(solution)/shard_map/ppermute | solution.py:697
  67.7 12.0 %collective-permute-done.9.refs_11_ = bf16[400,768]{1,0:T(8,128)(2,1)S(1)} collective-permute-done((bf16[400,768]{1,0:T(8,128)(2,1)}, bf16[400,768]{1,0:T(8,128)(2,1)S(1)}, u32[]{:S(2)}, u32[]{:S(2)}) %collective-permute-start.9) | collective-permute-done | bytes 614432 | tf_op jit(solution)/shard_map/ppermute | solution.py:697
  79.8 0.8 copy-done.18
  81.2 1.0 copy-done.17
  82.2 7.4 %all-to-all-done.refs_2_ = bf16[4,352,768]{2,1,0:T(8,128)(2,1)S(1)} async-done(((bf16[4,352,768]{2,1,0:T(8,128)(2,1)}), bf16[4,352,768]{2,1,0:T(8,128)(2,1)S(1)}, u32[]{:S(2)}, u32[]{:S(2)}) %all-to-all-start) | async-done | bytes 2162720 | tf_op jit(solution)/shard_map/all_to_all | solution.py:693
  89.6 1.4 %copy-done.16 = bf16[4,352,768]{2,1,0:T(8,128)(2,1)} copy-done((bf16[4,352,768]{2,1,0:T(8,128)(2,1)}, bf16[4,352,768]{2,1,0:T(8,128)(2,1)S(1)}, u32[]{:S(2)}) %copy-start.16) | copy-done | bytes 2162712
  91.0 12.5 %shard_map.154 = (bf16[352,384]{1,0:T(8,128)(2,1)}, bf16[352,384]{1,0:T(8,128)(2,1)}, bf16[352,384]{1,0:T(8,128)(2,1)}, bf16[352,384]{1,0:T(8,128)(2,1)}) custom-call(s32[4]{0:T(128)} %pad_add_fusion.refs_0_, s32[1]{0:T(128)} %get-tuple-element.26.refs_1_, bf16[4,352,768]{2,1,0:T(8,128)(2,1)} %copy-done.16, f32[768]{0:T(1024)} %refs_3_.5, f32[1,768]{1,0:T(1,128)} %refs_4_.1, ...), custom_call_target="tpu_custom_call" | custom-call | flops 1000000000 | bytes 3000000 | tf_op jit(solution)/shard_map/pallas_call | solution.py:184
  103.5 1.5 %collective-permute-start.15 = (bf16[352,384]{1,0:T(8,128)(2,1)}, bf16[352,384]{1,0:T(8,128)(2,1)S(1)}, u32[]{:S(2)}, u32[]{:S(2)}) collective-permute-start(bf16[352,384]{1,0:T(8,128)(2,1)} %get-tuple-element.42), channel_id=1, source_target_pairs={{0,2},{2,0},{1,3},{3,1},{4,6},{6,4},{5,7},{7,5},{8,10},{10,8},{9,1... | collective-permute-start | bytes 811016 | tf_op jit(solution)/shard_map/ppermute | solution.py:718
  105.5 1.5 %collective-permute-start.17 = (bf16[352,384]{1,0:T(8,128)(2,1)}, bf16[352,384]{1,0:T(8,128)(2,1)S(1)}, u32[]{:S(2)}, u32[]{:S(2)}) collective-permute-start(bf16[352,384]{1,0:T(8,128)(2,1)} %get-tuple-element.44), channel_id=1, source_target_pairs={{0,6},{2,4},{4,2},{6,0},{8,14},{10,12},{12,10},{14,8},{1,7},{3,5},... | collective-permute-start | bytes 811016 | tf_op jit(solution)/shard_map/ppermute | solution.py:717
  107.0 4.1 %collective-permute-done.15.refs_2_ = bf16[352,384]{1,0:T(8,128)(2,1)S(1)} collective-permute-done((bf16[352,384]{1,0:T(8,128)(2,1)}, bf16[352,384]{1,0:T(8,128)(2,1)S(1)}, u32[]{:S(2)}, u32[]{:S(2)}) %collective-permute-start.15) | collective-permute-done | bytes 270368 | tf_op jit(solution)/shard_map/ppermute | solution.py:718
  111.1 3.5 %collective-permute-done.16.refs_3_ = bf16[352,384]{1,0:T(8,128)(2,1)S(1)} collective-permute-done((bf16[352,384]{1,0:T(8,128)(2,1)}, bf16[352,384]{1,0:T(8,128)(2,1)S(1)}, u32[]{:S(2)}, u32[]{:S(2)}) %collective-permute-start.16) | collective-permute-done | bytes 270368 | tf_op jit(solution)/shard_map/ppermute | solution.py:716
  114.6 4.2 %collective-permute-done.17.refs_4_ = bf16[352,384]{1,0:T(8,128)(2,1)S(1)} collective-permute-done((bf16[352,384]{1,0:T(8,128)(2,1)}, bf16[352,384]{1,0:T(8,128)(2,1)S(1)}, u32[]{:S(2)}, u32[]{:S(2)}) %collective-permute-start.17) | collective-permute-done | bytes 270368 | tf_op jit(solution)/shard_map/ppermute | solution.py:717
  118.8 1.0 copy-done.13
  119.8 3.1 %shard_map.155 = bf16[1024,384]{1,0:T(8,128)(2,1)} custom-call(s32[1024,128]{1,0:T(8,128)S(1)} %get-tuple-element.25.refs_0_, bf16[352,384]{1,0:T(8,128)(2,1)S(1)} %copy-done.13, bf16[352,384]{1,0:T(8,128)(2,1)S(1)} %collective-permute-done.15.refs_2_, bf16[352,384]{1,0:T(8,128)(2,1)S(1)} %collective-permute-done.16.refs_3_, ...), custom_call_target="tpu_custom_call" | custom-call | flops 1000000000 | bytes 3000000 | tf_op jit(solution)/shard_map/pallas_call | solution.py:184
  (62 shorter events, 4.2 us)
Async XLA Ops:
  3.2 37.9 %collective-permute-start.4 = (bf16[400,768]{1,0:T(8,128)(2,1)}, bf16[400,768]{1,0:T(8,128)(2,1)S(1)}, u32[]{:S(2)}, u32[]{:S(2)}) collective-permute-start(bf16[400,768]{1,0:T(8,128)(2,1)} %shard_map.146.refs_6_), channel_id=1, source_target_pairs={{0,8},{4,12},{8,0},{12,4},{1,9},{5,13},{9,1},{13,5},{2,10},{6,14},... | collective-permute-start | bytes 1843208 | tf_op jit(solution)/shard_map/ppermute | solution.py:574
  7.3 9.7 %copy-start = (bf16[1,768,768]{2,1,0:T(8,128)(2,1)S(1)}, bf16[1,768,768]{2,1,0:T(8,128)(2,1)}, u32[]{:S(2)}) copy-start(bf16[1,768,768]{2,1,0:T(8,128)(2,1)} %refs_5_.3) | copy-start | bytes 3538948
  7.3 9.7 %copy-start.9 = (f32[1,768]{1,0:T(1,128)S(1)}, f32[1,768]{1,0:T(1,128)}, u32[]{:S(2)}) copy-start(f32[1,768]{1,0:T(1,128)} %refs_4_.1) | copy-start | bytes 9220
  7.3 9.7 %copy-start.10 = (s32[4]{0:T(128)S(1)}, s32[4]{0:T(128)}, u32[]{:S(2)}) copy-start(s32[4]{0:T(128)} %pad_add_fusion.refs_0_) | copy-start | bytes 52
  19.2 2.4 %copy-start.14 = (s32[1024]{0:T(1024)S(1)}, s32[1024]{0:T(1024)}, u32[]{:S(2)}) copy-start(s32[1024]{0:T(1024)} %param.25) | copy-start | bytes 12292
  19.2 2.4 %copy-start.15 = (s32[16]{0:T(128)S(1)}, s32[16]{0:T(128)}, u32[]{:S(2)}) copy-start(s32[16]{0:T(128)} %refs_1_.5) | copy-start | bytes 196
  19.2 11.8 %copy-start.2 = (bf16[1024,768]{1,0:T(8,128)(2,1)S(1)}, bf16[1024,768]{1,0:T(8,128)(2,1)}, u32[]{:S(2)}) copy-start(bf16[1024,768]{1,0:T(8,128)(2,1)} %refs_0_.3) | copy-start | bytes 4718596
  19.2 11.8 %copy-start.4 = (bf16[768,768]{1,0:T(8,128)(2,1)S(1)}, bf16[768,768]{1,0:T(8,128)(2,1)}, u32[]{:S(2)}) copy-start(bf16[768,768]{1,0:T(8,128)(2,1)} %refs_1_.8) | copy-start | bytes 3538948
  20.1 41.3 %collective-permute-start.8 = (bf16[784,768]{1,0:T(8,128)(2,1)S(1)}, bf16[784,768]{1,0:T(8,128)(2,1)}, u32[]{:S(2)}, u32[]{:S(2)}) collective-permute-start(bf16[784,768]{1,0:T(8,128)(2,1)S(1)} %shard_map.153), channel_id=1, source_target_pairs={{0,2},{2,0},{1,3},{3,1},{4,6},{6,4},{5,7},{7,5},{8,10},{10,8},{9,1... | collective-permute-start | bytes 3612680 | tf_op jit(solution)/shard_map/ppermute | solution.py:617
  21.7 1.7 %collective-permute-start = (bf16[144,768]{1,0:T(8,128)(2,1)S(1)}, bf16[144,768]{1,0:T(8,128)(2,1)S(1)}, u32[]{:S(2)}, u32[]{:S(2)}) collective-permute-start(bf16[144,768]{1,0:T(8,128)(2,1)S(1)} %copy-done.6), channel_id=1, source_target_pairs={{0,1},{1,0},{2,3},{3,2},{4,5},{5,4},{6,7},{7,6},{8,9},{9,8},{10,11... | collective-permute-start | bytes 663560 | tf_op jit(solution)/shard_map/ppermute | solution.py:604
  24.0 17.1 %collective-permute-start.1 = (bf16[144,384]{1,0:T(8,128)(2,1)S(1)}, bf16[144,384]{1,0:T(8,128)(2,1)S(1)}, u32[]{:S(2)}, u32[]{:S(2)}) collective-permute-start(bf16[144,384]{1,0:T(8,128)(2,1)S(1)} %shard_map.148.refs_2_), channel_id=1, source_target_pairs={{0,4},{4,8},{8,12},{1,5},{5,9},{9,13},{2,6},{6,10},{10,14},{3,7},{... | collective-permute-start | bytes 331784 | tf_op jit(solution)/shard_map/ppermute | solution.py:613
  27.5 13.6 %collective-permute-start.2 = (bf16[144,384]{1,0:T(8,128)(2,1)S(1)}, bf16[144,384]{1,0:T(8,128)(2,1)S(1)}, u32[]{:S(2)}, u32[]{:S(2)}) collective-permute-start(bf16[144,384]{1,0:T(8,128)(2,1)S(1)} %shard_map.148.refs_2_), channel_id=1, source_target_pairs={{0,8},{4,12},{1,9},{5,13},{2,10},{6,14},{3,11},{7,15},{16,24},{20,... | collective-permute-start | bytes 331784 | tf_op jit(solution)/shard_map/ppermute | solution.py:613
  29.7 11.3 %collective-permute-start.3 = (bf16[144,384]{1,0:T(8,128)(2,1)S(1)}, bf16[144,384]{1,0:T(8,128)(2,1)S(1)}, u32[]{:S(2)}, u32[]{:S(2)}) collective-permute-start(bf16[144,384]{1,0:T(8,128)(2,1)S(1)} %shard_map.148.refs_2_), channel_id=1, source_target_pairs={{0,12},{1,13},{2,14},{3,15},{16,28},{17,29},{18,30},{19,31}} | collective-permute-start | bytes 331784 | tf_op jit(solution)/shard_map/ppermute | solution.py:613
  31.1 2.3 %copy-start.7 = (bf16[1024,256]{1,0:T(8,128)(2,1)S(1)}, bf16[1024,256]{1,0:T(8,128)(2,1)}, u32[]{:S(2)}) copy-start(bf16[1024,256]{1,0:T(8,128)(2,1)} %get-tuple-element.28.refs_1_.refs_3_) | copy-start | bytes 1572868
  31.1 2.3 %copy-start.8 = (f32[12,1024]{1,0:T(8,128)S(1)}, f32[12,1024]{1,0:T(8,128)}, u32[]{:S(2)}) copy-start(f32[12,1024]{1,0:T(8,128)} %refs_2_.6) | copy-start | bytes 147460
  31.1 2.3 %copy-start.12 = (bf16[1024,768]{1,0:T(8,128)(2,1)S(1)}, bf16[1024,768]{1,0:T(8,128)(2,1)}, u32[]{:S(2)}) copy-start(bf16[1024,768]{1,0:T(8,128)(2,1)} %get-tuple-element.27.refs_0_) | copy-start | bytes 4718596
  41.0 3.6 %copy-start.5 = (bf16[768,768]{1,0:T(8,128)(2,1)S(1)}, bf16[768,768]{1,0:T(8,128)(2,1)}, u32[]{:S(2)}) copy-start(bf16[768,768]{1,0:T(8,128)(2,1)} %refs_9_.1) | copy-start | bytes 3538948
  41.0 3.6 %copy-start.11 = (f32[768]{0:T(1024)S(1)}, f32[768]{0:T(1024)}, u32[]{:S(2)}) copy-start(f32[768]{0:T(1024)} %refs_8_.1) | copy-start | bytes 9220
  41.1 25.6 %copy-start.3 = (bf16[400,768]{1,0:T(8,128)(2,1)}, bf16[400,768]{1,0:T(8,128)(2,1)S(1)}, u32[]{:S(2)}) copy-start(bf16[400,768]{1,0:T(8,128)(2,1)S(1)} %collective-permute-done.4.refs_5_.refs_8_) | copy-start | bytes 1843204
  41.2 20.2 %collective-permute-start.6 = (bf16[400,768]{1,0:T(8,128)(2,1)S(1)}, bf16[400,768]{1,0:T(8,128)(2,1)}, u32[]{:S(2)}, u32[]{:S(2)}) collective-permute-start(bf16[400,768]{1,0:T(8,128)(2,1)S(1)} %collective-permute-done.4.refs_5_.refs_8_), channel_id=1, source_target_pairs={{0,2},{2,0},{1,3},{3,1},{4,6},{6,4},{5,7},{7,5},{8,10},{10,8},{9,1... | collective-permute-start | bytes 1843208 | tf_op jit(solution)/shard_map/ppermute | solution.py:663
  41.8 19.6 %collective-permute-start.7 = (bf16[400,768]{1,0:T(8,128)(2,1)S(1)}, bf16[400,768]{1,0:T(8,128)(2,1)}, u32[]{:S(2)}, u32[]{:S(2)}) collective-permute-start(bf16[400,768]{1,0:T(8,128)(2,1)S(1)} %collective-permute-done.4.refs_5_.refs_8_), channel_id=1, source_target_pairs={{0,16},{16,0},{1,17},{17,1},{2,18},{18,2},{3,19},{19,3},{4,20},{20... | collective-permute-start | bytes 1843208 | tf_op jit(solution)/shard_map/ppermute | solution.py:664
  43.3 1.3 %collective-permute-start.5 = (bf16[128,384]{1,0:T(8,128)(2,1)S(1)}, bf16[128,384]{1,0:T(8,128)(2,1)S(1)}, u32[]{:S(2)}, u32[]{:S(2)}) collective-permute-start(bf16[128,384]{1,0:T(8,128)(2,1)S(1)} %shard_map.151.refs_5_), channel_id=1, source_target_pairs={{0,1},{1,0},{2,3},{3,2},{4,5},{5,4},{6,7},{7,6},{8,9},{9,8},{10,11... | collective-permute-start | bytes 294920 | tf_op jit(solution)/shard_map/ppermute | solution.py:665
  61.4 28.3 %all-to-all-start = ((bf16[4,352,768]{2,1,0:T(8,128)(2,1)}), bf16[4,352,768]{2,1,0:T(8,128)(2,1)S(1)}, u32[]{:S(2)}, u32[]{:S(2)}) async-start(bf16[4,352,768]{2,1,0:T(8,128)(2,1)} %shard_map.152), calls=%async_computation | async-start | bytes 4325376 | tf_op jit(solution)/shard_map/all_to_all | solution.py:693
  65.2 14.5 %collective-permute-start.9 = (bf16[400,768]{1,0:T(8,128)(2,1)}, bf16[400,768]{1,0:T(8,128)(2,1)S(1)}, u32[]{:S(2)}, u32[]{:S(2)}) collective-permute-start(bf16[400,768]{1,0:T(8,128)(2,1)} %collective-permute-done.6.refs_10_), channel_id=1, source_target_pairs={{0,16},{16,0},{1,17},{17,1},{2,18},{18,2},{3,19},{19,3},{4,20},{20... | collective-permute-start | bytes 1843208 | tf_op jit(solution)/shard_map/ppermute | solution.py:697
  66.7 13.1 %collective-permute-start.10 = (bf16[784,768]{1,0:T(8,128)(2,1)}, bf16[784,768]{1,0:T(8,128)(2,1)S(1)}, u32[]{:S(2)}, u32[]{:S(2)}) collective-permute-start(bf16[784,768]{1,0:T(8,128)(2,1)} %collective-permute-done.8.refs_7_), channel_id=1, source_target_pairs={{0,1},{1,0},{2,3},{3,2},{4,5},{5,4},{6,7},{7,6},{8,9},{9,8},{10,11... | collective-permute-start | bytes 3612680 | tf_op jit(solution)/shard_map/ppermute | solution.py:699
  66.7 13.0 %collective-permute-start.11 = (bf16[400,768]{1,0:T(8,128)(2,1)S(1)}, bf16[400,768]{1,0:T(8,128)(2,1)S(1)}, u32[]{:S(2)}, u32[]{:S(2)}) collective-permute-start(bf16[400,768]{1,0:T(8,128)(2,1)S(1)} %collective-permute-done.4.refs_5_.refs_8_), channel_id=1, source_target_pairs={{0,1},{1,0},{2,3},{3,2},{4,5},{5,4},{6,7},{7,6},{8,9},{9,8},{10,11... | collective-permute-start | bytes 1843208 | tf_op jit(solution)/shard_map/ppermute | solution.py:699
  67.2 12.5 %collective-permute-start.12 = (bf16[400,768]{1,0:T(8,128)(2,1)}, bf16[400,768]{1,0:T(8,128)(2,1)S(1)}, u32[]{:S(2)}, u32[]{:S(2)}) collective-permute-start(bf16[400,768]{1,0:T(8,128)(2,1)} %collective-permute-done.7.refs_9_), channel_id=1, source_target_pairs={{0,1},{1,0},{2,3},{3,2},{4,5},{5,4},{6,7},{7,6},{8,9},{9,8},{10,11... | collective-permute-start | bytes 1843208 | tf_op jit(solution)/shard_map/ppermute | solution.py:699
  67.2 12.5 %collective-permute-start.13 = (bf16[400,768]{1,0:T(8,128)(2,1)}, bf16[400,768]{1,0:T(8,128)(2,1)S(1)}, u32[]{:S(2)}, u32[]{:S(2)}) collective-permute-start(bf16[400,768]{1,0:T(8,128)(2,1)} %collective-permute-done.6.refs_10_), channel_id=1, source_target_pairs={{0,1},{1,0},{2,3},{3,2},{4,5},{5,4},{6,7},{7,6},{8,9},{9,8},{10,11... | collective-permute-start | bytes 1843208 | tf_op jit(solution)/shard_map/ppermute | solution.py:699
  79.7 2.5 %collective-permute-start.14 = (bf16[400,768]{1,0:T(8,128)(2,1)S(1)}, bf16[400,768]{1,0:T(8,128)(2,1)}, u32[]{:S(2)}, u32[]{:S(2)}) collective-permute-start(bf16[400,768]{1,0:T(8,128)(2,1)S(1)} %collective-permute-done.9.refs_11_), channel_id=1, source_target_pairs={{0,1},{1,0},{2,3},{3,2},{4,5},{5,4},{6,7},{7,6},{8,9},{9,8},{10,11... | collective-permute-start | bytes 1843208 | tf_op jit(solution)/shard_map/ppermute | solution.py:699
  103.5 7.7 %collective-permute-start.15 = (bf16[352,384]{1,0:T(8,128)(2,1)}, bf16[352,384]{1,0:T(8,128)(2,1)S(1)}, u32[]{:S(2)}, u32[]{:S(2)}) collective-permute-start(bf16[352,384]{1,0:T(8,128)(2,1)} %get-tuple-element.42), channel_id=1, source_target_pairs={{0,2},{2,0},{1,3},{3,1},{4,6},{6,4},{5,7},{7,5},{8,10},{10,8},{9,1... | collective-permute-start | bytes 811016 | tf_op jit(solution)/shard_map/ppermute | solution.py:718
  105.0 9.6 %collective-permute-start.16 = (bf16[352,384]{1,0:T(8,128)(2,1)}, bf16[352,384]{1,0:T(8,128)(2,1)S(1)}, u32[]{:S(2)}, u32[]{:S(2)}) collective-permute-start(bf16[352,384]{1,0:T(8,128)(2,1)} %get-tuple-element.43), channel_id=1, source_target_pairs={{0,4},{4,0},{8,12},{12,8},{1,5},{5,1},{9,13},{13,9},{2,6},{6,2},{1... | collective-permute-start | bytes 811016 | tf_op jit(solution)/shard_map/ppermute | solution.py:716
  105.5 13.2 %collective-permute-start.17 = (bf16[352,384]{1,0:T(8,128)(2,1)}, bf16[352,384]{1,0:T(8,128)(2,1)S(1)}, u32[]{:S(2)}, u32[]{:S(2)}) collective-permute-start(bf16[352,384]{1,0:T(8,128)(2,1)} %get-tuple-element.44), channel_id=1, source_target_pairs={{0,6},{2,4},{4,2},{6,0},{8,14},{10,12},{12,10},{14,8},{1,7},{3,5},... | collective-permute-start | bytes 811016 | tf_op jit(solution)/shard_map/ppermute | solution.py:717
  (9 other events, 10.1 us)
where the time goes:
time: 123 us
  Pallas kernels  51.3 us (42%)
  waiting for transfers between devices  38.9 us (32%)
  starting transfers between devices  24.7 us (20%)
  local copies, waits for them, and re-layouts  7.04 us (6%)
    pallas_call x11, Pallas kernels, call(): return lambda *args: run(*args, *after)  51.3 us
    ppermute x1, waiting for transfers between devices, fast(): far_xy = lax.ppermute(far_x, 'groups', swap)  12 us
    all_to_all x1, waiting for transfers between devices, fast(): lax.all_to_all(blocks, ('tm', 'mp'), 0, 0, axis_index_groups=squares, til...  7.4 us
    unnamed x44, local copies, waits for them, and re-layouts  7.04 us
    ppermute x3, starting transfers between devices, fast(): lax.ppermute(chip, 'tm', [(i, i + hop) for i in range(shard_count - hop)])  7.03 us
    ppermute x1, waiting for transfers between devices, fast(): far_x = lax.ppermute(far, 'mp', swap)  6.43 us
    ppermute x1, waiting for transfers between devices, fast(): back_other = lax.ppermute(other, ('tm', 'mp'), near_x)  4.17 us
    ppermute x1, waiting for transfers between devices, fast(): back_l = lax.ppermute(other_l, 'mp', swap)  4.1 us
  transfers between devices with their start and end apart: 19, of which 7 were waited for; matrix products, arithmetic and copies ran while one was open for 0% of the time, Pallas kernels for 27%

commit v1 on v0

--- a/solution.py
+++ b/solution.py
@@ -333,7 +333,8 @@
     run[...] += jnp.broadcast_to(last, run.shape)
 
 
-def norm_kernel(info, y, gate, bc, past, mine, other, before, gain, w_out, slot, out, carry, all_rows):
+def norm_kernel(info, y, gate, bc, past, mine, other, before, gain, w_out, slot, *refs):
+    outs, (carry, all_rows) = refs[:4], refs[4:]
     step_id = pl.program_id(0)
     rows, channels = y.shape
     heads = past.shape[1]
@@ -358,18 +359,21 @@
 
     @pl.when(step_id == pl.num_programs(0) - 1)
     def _():
-        count = out.shape[1]
-        here = 2 * (info[0] & 1) + info[1]
-        for place in range(4):
-            first = (place ^ here) * count
-            pick = ones_where(slot[...] == iota((count, slot.shape[1]), 0) + first)
-            out[place] = dot(pick, all_rows[...]).astype(BF16)
+        for number, out in enumerate(outs):
+            count = out.shape[0]
+            pick = ones_where(slot[...] == iota((count, slot.shape[1]), 0) + number * count)
+            out[...] = dot(pick, all_rows[...]).astype(BF16)
 
 
 def mixed(term_1, term_2, gain):
     total = term_1[...].astype(F32) + term_2[...].astype(F32)
     mean = jnp.mean(total * total, axis=1, keepdims=True)
     return (total * lax.rsqrt(mean + 1e-05) * gain[...][None, :]).astype(BF16)
+
+
+def mix_kernel(keep, recv, term_1, term_2, gain, away, local):
+    away[...] = mixed(term_1, term_2, gain)
+    local[...] = mixed(keep, recv, gain)
 
 
 def route_kernel(cold, info, shard, port, slot_o, column_o, flag_o):
@@ -402,73 +406,77 @@
     column_o[...] = wide.T.astype(jnp.int32)
 
 
-def readout_kernel(cold, info, flag, terms, gain, bias, w_up, w_down, *refs):
-    pieces = refs[:10]
-    same_o, other_o, same_l_o, other_l_o, up, down, extra, total, sems = refs[10:]
-    width = up.shape[1]
-    part = width // 4
-    copies = [[] for _ in range(4)]
-    used = 0
-
-    def start(bank, source, target):
-        nonlocal used
-        copy = pltpu.make_async_copy(source, target, sems.at[used])
-        copy.start()
-        copies[bank].append(copy)
-        used += 1
-
-    start(0, w_up.at[0], up.at[0])
-    start(0, w_down.at[0], down.at[0])
-    for core in (0, 1):
-        here = (info[3] ^ core) * 2
-        at = pl.ds(pl.multiple_of(here * part, 2 * part), 2 * part)
-        piece = pieces[5 * core]
-        start(1, piece.at[pl.ds(0, 2 * part)], up.at[1, at])
-        start(1, piece.at[pl.ds(2 * part, 2 * part)], down.at[1, at])
-        for number, bank in enumerate((2, 2, 3, 3)):
-            piece = pieces[5 * core + 1 + number]
-            first = here + (info[2] ^ (number % 2))
-            at = pl.ds(pl.multiple_of(first * part, part), part)
-            start(bank, piece.at[pl.ds(0, part)], up.at[bank, at])
-            start(bank, piece.at[pl.ds(part, part)], down.at[bank, at])
-    start(1, pieces[0].at[pl.ds(4 * part, TILE)], extra.at[1])
-    start(2, pieces[1].at[pl.ds(2 * part, TILE)], extra.at[2])
-    start(3, pieces[3].at[pl.ds(2 * part, TILE)], extra.at[3])
-
-    odd = info[0] & 1
-    away = mixed(terms.at[2 - 2 * odd], terms.at[3 - 2 * odd], gain)
-    local = mixed(terms.at[2 * odd], terms.at[2 * odd + 1], gain)
+def starter(sems):
+    copies = []
+
+    def start(source, target):
+        copies.append(pltpu.make_async_copy(source, target, sems.at[len(copies)]))
+        copies[-1].start()
+
+    return copies, start
+
+
+def quarters(info, pieces, start, up, down, bank):
+    part = up.shape[1] // 4
+    for number, piece in enumerate(pieces):
+        first = (info[3] ^ (number // 2)) * 2 + (info[2] ^ (number % 2))
+        at = pl.ds(pl.multiple_of(first * part, part), part)
+        start(piece.at[pl.ds(0, part)], up.at[bank, at])
+        start(piece.at[pl.ds(part, part)], down.at[bank, at])
+
+
+def weights_kernel(info, bias, w_up, w_down, own, own_s, far_1, far_2, far_1s, far_2s, up, down, shift, extra, sems):
+    part = up.shape[1] // 4
+    copies, start = starter(sems)
+    start(w_up.at[0], up.at[0])
+    start(w_down.at[0], down.at[0])
+    for core, piece in enumerate((own, own_s)):
+        at = pl.ds(pl.multiple_of((info[3] ^ core) * 2 * part, 2 * part), 2 * part)
+        start(piece.at[pl.ds(0, 2 * part)], up.at[1, at])
+        start(piece.at[pl.ds(2 * part, 2 * part)], down.at[1, at])
+    quarters(info, (far_1, far_2, far_1s, far_2s), start, up, down, 2)
+    start(own.at[pl.ds(4 * part, TILE)], extra.at[0])
+    start(far_1.at[pl.ds(2 * part, TILE)], extra.at[1])
+    for copy in copies:
+        copy.wait()
+    rows = [bias[...]] + [jnp.sum(extra[i].astype(F32), axis=0, keepdims=True) for i in range(2)]
+    shift[...] = jnp.concatenate(rows + rows[:1], axis=0)
+
+
+def readout_kernel(cold, info, flag, away, local, shift, up, down, *refs):
+    pieces = refs[:4]
+    same_o, other_o, same_l_o, other_l_o, total, up_3, down_3, extra, sems = refs[4:]
+    copies, start = starter(sems)
+    quarters(info, pieces, start, up_3, down_3, 0)
+    start(pieces[0].at[pl.ds(up.shape[1] // 2, TILE)], extra)
     count = away.shape[0]
 
-    def run(lo, hi, bank, first):
+    def run(lo, hi, bank):
         size = hi - lo
         x = jnp.concatenate([away[lo:hi], local[lo:hi]], axis=0)
         out = None
         for half in (0, 1):
-            if first:
-                for copy in copies[bank + half]:
+            if bank + half == 3:
+                for copy in copies:
                     copy.wait()
-            if bank + half == 0:
-                shift = bias[...]
+                v = dot(x, up_3[0]) + jnp.sum(extra[...].astype(F32), axis=0, keepdims=True)
             else:
-                shift = jnp.sum(extra[bank + half].astype(F32), axis=0, keepdims=True)
-            v = dot(x, up[bank + half]) + shift
+                v = dot(x, up[bank + half]) + shift[bank + half : bank + half + 1, :]
             hidden = (0.5 * v * (1.0 + jnp.tanh(0.7978845608028654 * (v + 0.044715 * v * v * v)))).astype(BF16)
-            y = dot(hidden, down[bank + half])
+            y = dot(hidden, down_3[0] if bank + half == 3 else down[bank + half])
             out = y if half == 0 else out + y
         total[0, lo:hi, :] = out[:size]
         total[1, lo:hi, :] = out[size:]
 
-    run(0, cold, 0, True)
-    run(count - cold, count, 2, True)
-
     @pl.when(flag[0] == 0)
     def _():
-        run(cold, count - cold, 0, False)
+        run(0, count - cold, 0)
+        run(count - cold, count, 2)
 
     @pl.when(flag[0] != 0)
     def _():
-        run(cold, count - cold, 2, False)
+        run(0, cold, 0)
+        run(cold, count, 2)
 
     place = info[1]
     side = same_o.shape[1]
@@ -666,7 +674,7 @@
 
     blocks = call(
         norm_kernel,
-        arr((4, count, width), BF16),
+        (arr((count, width), BF16),) * 4,
         room=24,
         micros=0.1,
         grid=grid,
@@ -683,36 +691,54 @@
             fixed(w_out.shape),
             fixed(slot.shape),
         ],
-        out_specs=fixed((4, count, width)),
+        out_specs=(fixed((count, width)),) * 4,
         scratch_shapes=[pltpu.VMEM((nstate, channels), BF16), pltpu.VMEM((length, width), BF16)],
     )(info, y, gate, bc, past, carry, carry_beside, beside, norm_gain, w_out, slot)
     near = [(i, i ^ 1) for i in range(shard_count)]
     near_x = [(2 * i + j, 2 * (i ^ 1) + (j ^ 1)) for i in range(shard_count) for j in range(2)]
-    squares = [[4 * i + j for j in range(4)] for i in range(shard_count // 2)]
-    blocks = tie(tie(tie(blocks, far_x), far_y), own)
-    terms = lax.all_to_all(
-        blocks, ("tm", "mp"), 0, 0, axis_index_groups=squares, tiled=True
-    )
-    own, far, far_y, far_x = (tie(a, blocks) for a in (own, far, far_y, far_x))
+    keep, beside_rows, same, other = blocks
+    for piece in (far_x, far_y, own):
+        beside_rows, same, other = (tie(a, piece) for a in (beside_rows, same, other))
+    terms = (
+        keep,
+        lax.ppermute(beside_rows, "mp", swap),
+        lax.ppermute(same, "tm", near),
+        lax.ppermute(other, ("tm", "mp"), near_x),
+    )
+    own, far, far_y, far_x = (tie(a, keep) for a in (own, far, far_y, far_x))
     far_xy = lax.ppermute(far_x, "groups", swap)
-    firsts = [own, far, far_y, far_x, far_xy]
-    pieces = firsts + [lax.ppermute(a, "sub", swap) for a in firsts]
-
+    away, local = call(
+        mix_kernel,
+        (arr((count, width), BF16),) * 2,
+        micros=0.1,
+        in_specs=[VMEM] * 5,
+        out_specs=(VMEM,) * 2,
+    )(*terms, mix_gain)
+    own_s, far_s, far_ys, far_xs = (lax.ppermute(a, "sub", swap) for a in (own, far, far_y, far_x))
+    far_xys = lax.ppermute(tie(far_xy, away), "sub", swap)
+
+    up, down, shift = call(
+        weights_kernel,
+        (arr((3, width, width), BF16), arr((3, width, width), BF16), arr((4, width), F32)),
+        micros=0.1,
+        in_specs=[SMEM, VMEM] + [ANY] * 8,
+        out_specs=(VMEM,) * 3,
+        scratch_shapes=[pltpu.VMEM((2, TILE, width), BF16), pltpu.SemaphoreType.DMA((16,))],
+    )(info, b_up, w_up, w_down, own, own_s, far, far_y, far_s, far_ys)
     same, other, same_l, other_l = call(
         lambda *refs: readout_kernel(cold, *refs),
         (arr((count, side), BF16),) * 4,
-        room=60,
-        micros=1,
-        in_specs=[SMEM, SMEM] + [VMEM] * 3 + [ANY] * 12,
+        micros=9,
+        in_specs=[SMEM, SMEM] + [VMEM] * 5 + [ANY] * 4,
         out_specs=(VMEM,) * 4,
         scratch_shapes=[
-            pltpu.VMEM((4, width, width), BF16),
-            pltpu.VMEM((4, width, width), BF16),
-            pltpu.VMEM((4, TILE, width), BF16),
             pltpu.VMEM((2, count, width), F32),
-            pltpu.SemaphoreType.DMA((29,)),
+            pltpu.VMEM((1, width, width), BF16),
+            pltpu.VMEM((1, width, width), BF16),
+            pltpu.VMEM((TILE, width), BF16),
+            pltpu.SemaphoreType.DMA((9,)),
         ],
-    )(info, flag, terms, mix_gain, b_up, w_up, w_down, *pieces)
+    )(info, flag, away, local, shift, up, down, far_x, far_xy, far_xs, far_xys)
     back_same = lax.ppermute(same, "tm", near)
     back_other = lax.ppermute(other, ("tm", "mp"), near_x)
     back_l = lax.ppermute(other_l, "mp", swap)

time: 123 us -> 120 us (0.976)
  waiting for transfers between devices: 38.9 us -> 45.7 us
  local copies, waits for them, and re-layouts: 7.04 us -> 2.26 us
  Pallas kernels: 51.3 us -> 46.8 us
    ppermute x5 -> x8, waiting for transfers between devices: 0.01 us -> 24.8 us  [the longest x1 11.1 us: fast(): lax.ppermute(beside_rows, 'mp', swap)]
    ppermute x1, waiting for transfers between devices: 12 us -> 0.01 us  [fast(): far_xy = lax.ppermute(far_x, 'groups', swap)]
    all_to_all x1 -> x0, waiting for transfers between devices: 7.4 us -> none  [fast(): lax.all_to_all(blocks, ('tm', 'mp'), 0, 0, axis_index_groups=squares, til...]
    unnamed x44 -> x32, local copies, waits for them, and re-layouts: 7.04 us -> 2.26 us
    pallas_call x11 -> x13, Pallas kernels: 51.3 us -> 46.8 us  [call(): return lambda *args: run(*args, *after)]
    all_to_all x1 -> x0, starting transfers between devices: 3.77 us -> none  [fast(): lax.all_to_all(blocks, ('tm', 'mp'), 0, 0, axis_index_groups=squares, til...]
    ppermute x5 -> x8, starting transfers between devices: 1.02 us -> 4.14 us  [the longest x1 1.57 us: fast(): lax.ppermute(same, 'tm', near)]
  transfers between devices with their start and end apart: 19 -> 21, of which waited for: 7 -> 9; matrix products, arithmetic and copies ran while one was open for 0% -> 0% of each run, Pallas kernels for 27% -> 29%
where the time goes in v1:
time: 120 us
  Pallas kernels  46.8 us (39%)
  waiting for transfers between devices  45.7 us (38%)
  starting transfers between devices  24 us (20%)
  local copies, waits for them, and re-layouts  2.26 us (2%)
    pallas_call x13, Pallas kernels, call(): return lambda *args: run(*args, *after)  46.8 us
    ppermute x1, waiting for transfers between devices, fast(): lax.ppermute(beside_rows, 'mp', swap)  11.1 us
    ppermute x1, waiting for transfers between devices, fast(): lax.ppermute(other, ('tm', 'mp'), near_x)  10.8 us
    ppermute x1, waiting for transfers between devices, fast(): far_x = lax.ppermute(far, 'mp', swap)  7.61 us
    ppermute x3, starting transfers between devices, fast(): lax.ppermute(chip, 'tm', [(i, i + hop) for i in range(shard_count - hop)])  7.02 us
    ppermute x1, waiting for transfers between devices, fast(): back_l = lax.ppermute(other_l, 'mp', swap)  5.03 us
    ppermute x1, waiting for transfers between devices, fast(): back_other = lax.ppermute(other, ('tm', 'mp'), near_x)  4.63 us
    ppermute x1, starting transfers between devices, fast(): far = lax.ppermute(share, 'tm', [(i, i ^ 2) for i in range(shard_count)])  4.1 us
  transfers between devices with their start and end apart: 21, of which 9 were waited for; matrix products, arithmetic and copies ran while one was open for 0% of the time, Pallas kernels for 29%

profile of v1, /device:TPU:0, one launch (start us, length us, event | category | flops | bytes accessed | tf_op | source)
XLA Modules:
  0.0 119.8 jit_solution(1911093184863127417)
XLA Ops:
  0.6 2.6 %shard_map.146.refs_6_ = bf16[400,768]{1,0:T(8,128)(2,1)} custom-call(s32[4]{0:T(128)} %pad_add_fusion.refs_0_, f32[1,768]{1,0:T(1,128)} %refs_1_.11, bf16[1,768,768]{2,1,0:T(8,128)(2,1)} %refs_2_.9, bf16[1,768,768]{2,1,0:T(8,128)(2,1)} %refs_3_.5), custom_call_target="tpu_custom_call" | custom-call | flops 100000000 | bytes 300000 | tf_op jit(solution)/shard_map/pallas_call | solution.py:184
  3.2 4.1 %collective-permute-start.4 = (bf16[400,768]{1,0:T(8,128)(2,1)}, bf16[400,768]{1,0:T(8,128)(2,1)S(1)}, u32[]{:S(2)}, u32[]{:S(2)}) collective-permute-start(bf16[400,768]{1,0:T(8,128)(2,1)} %shard_map.146.refs_6_), channel_id=1, source_target_pairs={{0,8},{4,12},{8,0},{12,4},{1,9},{5,13},{9,1},{13,5},{2,10},{6,14},... | collective-permute-start | bytes 1843208 | tf_op jit(solution)/shard_map/ppermute | solution.py:582
  7.3 9.7 %shard_map.147 = (bf16[1024,768]{1,0:T(8,128)(2,1)}, bf16[1024,256]{1,0:T(8,128)(2,1)}, bf16[144,768]{1,0:T(8,128)(2,1)}) custom-call(bf16[1024,768]{1,0:T(8,128)(2,1)} %refs_0_.3, bf16[768,768]{1,0:T(8,128)(2,1)} %refs_1_.8, bf16[768,256]{1,0:T(8,128)(2,1)} %refs_2_.6, bf16[12,768]{1,0:T(8,128)(2,1)} %bitcast.8, f32[1,12]{1,0:T(1,128)} %bitcast.9, ...), custom_call_target="tpu_custom_call" | custom-call | flops 100000000 | bytes 300000 | tf_op jit(solution)/shard_map/pallas_call | solution.py:184
  17.0 1.3 %copy-done.1 = bf16[1,768,768]{2,1,0:T(8,128)(2,1)S(1)} copy-done((bf16[1,768,768]{2,1,0:T(8,128)(2,1)S(1)}, bf16[1,768,768]{2,1,0:T(8,128)(2,1)}, u32[]{:S(2)}) %copy-start.1) | copy-done | bytes 1179672
  18.3 0.9 copy-done.6
  19.3 0.8 shard_map.153
  20.1 1.6 %collective-permute-start.8 = (bf16[784,768]{1,0:T(8,128)(2,1)S(1)}, bf16[784,768]{1,0:T(8,128)(2,1)S(1)}, u32[]{:S(2)}, u32[]{:S(2)}) collective-permute-start(bf16[784,768]{1,0:T(8,128)(2,1)S(1)} %shard_map.153), channel_id=1, source_target_pairs={{0,2},{2,0},{1,3},{3,1},{4,6},{6,4},{5,7},{7,5},{8,10},{10,8},{9,1... | collective-permute-start | bytes 3612680 | tf_op jit(solution)/shard_map/ppermute | solution.py:625
  21.7 1.7 %shard_map.145 = (s32[1,1024]{1,0:T(1,128)S(1)}, s32[1024,128]{1,0:T(8,128)S(1)}, s32[1]{0:T(128)}) custom-call(s32[4]{0:T(128)S(1)} %copy-done.10, s32[16]{0:T(128)S(1)} %copy-done.15, s32[1,1024]{1,0:T(1,128)S(1)} %bitcast.7), custom_call_target="tpu_custom_call" | custom-call | flops 100000000 | bytes 300000 | tf_op jit(solution)/shard_map/pallas_call | solution.py:184
  24.0 3.5 %collective-permute-start.1 = (bf16[144,384]{1,0:T(8,128)(2,1)S(1)}, bf16[144,384]{1,0:T(8,128)(2,1)S(1)}, u32[]{:S(2)}, u32[]{:S(2)}) collective-permute-start(bf16[144,384]{1,0:T(8,128)(2,1)S(1)} %shard_map.148.refs_2_), channel_id=1, source_target_pairs={{0,4},{4,8},{8,12},{1,5},{5,9},{9,13},{2,6},{6,10},{10,14},{3,7},{... | collective-permute-start | bytes 331784 | tf_op jit(solution)/shard_map/ppermute | solution.py:621
  27.5 2.2 %collective-permute-start.2 = (bf16[144,384]{1,0:T(8,128)(2,1)S(1)}, bf16[144,384]{1,0:T(8,128)(2,1)S(1)}, u32[]{:S(2)}, u32[]{:S(2)}) collective-permute-start(bf16[144,384]{1,0:T(8,128)(2,1)S(1)} %shard_map.148.refs_2_), channel_id=1, source_target_pairs={{0,8},{4,12},{1,9},{5,13},{2,10},{6,14},{3,11},{7,15},{16,24},{20,... | collective-permute-start | bytes 331784 | tf_op jit(solution)/shard_map/ppermute | solution.py:621
  29.7 1.3 %collective-permute-start.3 = (bf16[144,384]{1,0:T(8,128)(2,1)S(1)}, bf16[144,384]{1,0:T(8,128)(2,1)S(1)}, u32[]{:S(2)}, u32[]{:S(2)}) collective-permute-start(bf16[144,384]{1,0:T(8,128)(2,1)S(1)} %shard_map.148.refs_2_), channel_id=1, source_target_pairs={{0,12},{1,13},{2,14},{3,15},{16,28},{17,29},{18,30},{19,31}} | collective-permute-start | bytes 331784 | tf_op jit(solution)/shard_map/ppermute | solution.py:621
  31.1 2.3 %shard_map.149.refs_3_.refs_2_ = f32[1024,768]{1,0:T(8,128)S(1)} custom-call(bf16[1024,768]{1,0:T(8,128)(2,1)S(1)} %copy-done.3, bf16[768,768]{1,0:T(8,128)(2,1)S(1)} %copy-done.5, bf16[144,384]{1,0:T(8,128)(2,1)S(1)} %shard_map.148.refs_2_, s32[1,1024]{1,0:T(1,128)S(1)} %get-tuple-element.46.refs_3_.refs_4_.refs_10_), custom_call_target="tpu_custom_call" | custom-call | flops 100000000 | bytes 300000 | tf_op jit(solution)/shard_map/pallas_call | solution.py:184
  33.4 7.6 %shard_map.150 = (f32[1024,768]{1,0:T(8,128)S(1)}, f32[1024,12]{1,0:T(8,128)S(1)}) custom-call(bf16[1024,768]{1,0:T(8,128)(2,1)S(1)} %copy-done.13, bf16[1024,256]{1,0:T(8,128)(2,1)S(1)} %copy-done.7, f32[12,1024]{1,0:T(8,128)S(1)} %copy-done.8, f32[1024,768]{1,0:T(8,128)S(1)} %shard_map.149.refs_3_.refs_2_), custom_call_target="tpu_custom_call" | custom-call | flops 2000000000 | bytes 6000000 | tf_op jit(solution)/shard_map/pallas_call | solution.py:184
  41.8 1.5 %collective-permute-start.7 = (bf16[400,768]{1,0:T(8,128)(2,1)S(1)}, bf16[400,768]{1,0:T(8,128)(2,1)S(1)}, u32[]{:S(2)}, u32[]{:S(2)}) collective-permute-start(bf16[400,768]{1,0:T(8,128)(2,1)S(1)} %collective-permute-done.4.refs_5_.refs_6_), channel_id=1, source_target_pairs={{0,16},{16,0},{1,17},{17,1},{2,18},{18,2},{3,19},{19,3},{4,20},{20... | collective-permute-start | bytes 1843208 | tf_op jit(solution)/shard_map/ppermute | solution.py:672
  43.3 1.3 %collective-permute-done.5.refs_6_ = bf16[128,384]{1,0:T(8,128)(2,1)S(1)} collective-permute-done((bf16[128,384]{1,0:T(8,128)(2,1)S(1)}, bf16[128,384]{1,0:T(8,128)(2,1)S(1)}, u32[]{:S(2)}, u32[]{:S(2)}) %collective-permute-start.5) | collective-permute-done | bytes 98336 | tf_op jit(solution)/shard_map/ppermute | solution.py:673
  44.6 9.1 %shard_map.152 = (bf16[352,768]{1,0:T(8,128)(2,1)S(1)}, bf16[352,768]{1,0:T(8,128)(2,1)S(1)}, bf16[352,768]{1,0:T(8,128)(2,1)S(1)}, bf16[352,768]{1,0:T(8,128)(2,1)S(1)}) custom-call(s32[4]{0:T(128)S(1)} %copy-done.10, f32[1024,768]{1,0:T(8,128)S(1)} %get-tuple-element.47.refs_1_, f32[1024,768]{1,0:T(8,128)S(1)} %shard_map.149.refs_3_.refs_2_, ...), custom_call_target="tpu_custom_call" | custom-call | flops 100000000 | bytes 300000 | tf_op jit(solution)/shard_map/pallas_call | solution.py:184
  53.7 7.6 %collective-permute-done.6.refs_7_ = bf16[400,768]{1,0:T(8,128)(2,1)S(1)} collective-permute-done((bf16[400,768]{1,0:T(8,128)(2,1)S(1)}, bf16[400,768]{1,0:T(8,128)(2,1)S(1)}, u32[]{:S(2)}, u32[]{:S(2)}) %collective-permute-start.6) | collective-permute-done | bytes 614432 | tf_op jit(solution)/shard_map/ppermute | solution.py:671
  61.3 1.5 %collective-permute-start.15 = (bf16[400,768]{1,0:T(8,128)(2,1)S(1)}, bf16[400,768]{1,0:T(8,128)(2,1)S(1)}, u32[]{:S(2)}, u32[]{:S(2)}) collective-permute-start(bf16[400,768]{1,0:T(8,128)(2,1)S(1)} %collective-permute-done.6.refs_7_), channel_id=1, source_target_pairs={{0,16},{16,0},{1,17},{17,1},{2,18},{18,2},{3,19},{19,3},{4,20},{20... | collective-permute-start | bytes 1843208 | tf_op jit(solution)/shard_map/ppermute | solution.py:709
  62.8 1.6 %collective-permute-start.9 = (bf16[352,768]{1,0:T(8,128)(2,1)S(1)}, bf16[352,768]{1,0:T(8,128)(2,1)S(1)}, u32[]{:S(2)}, u32[]{:S(2)}) collective-permute-start(bf16[352,768]{1,0:T(8,128)(2,1)S(1)} %get-tuple-element.54), channel_id=1, source_target_pairs={{0,2},{2,0},{1,3},{3,1},{4,6},{6,4},{5,7},{7,5},{8,10},{10,8},{9,1... | collective-permute-start | bytes 1622024 | tf_op jit(solution)/shard_map/ppermute | solution.py:704
  64.4 1.6 %collective-permute-start.10 = (bf16[352,768]{1,0:T(8,128)(2,1)S(1)}, bf16[352,768]{1,0:T(8,128)(2,1)S(1)}, u32[]{:S(2)}, u32[]{:S(2)}) collective-permute-start(bf16[352,768]{1,0:T(8,128)(2,1)S(1)} %get-tuple-element.58), channel_id=1, source_target_pairs={{0,4},{4,0},{8,12},{12,8},{1,5},{5,1},{9,13},{13,9},{2,6},{6,2},{1... | collective-permute-start | bytes 1622024 | tf_op jit(solution)/shard_map/ppermute | solution.py:705
  66.4 11.1 %collective-permute-done.9.refs_1_ = bf16[352,768]{1,0:T(8,128)(2,1)S(1)} collective-permute-done((bf16[352,768]{1,0:T(8,128)(2,1)S(1)}, bf16[352,768]{1,0:T(8,128)(2,1)S(1)}, u32[]{:S(2)}, u32[]{:S(2)}) %collective-permute-start.9) | collective-permute-done | bytes 540704 | tf_op jit(solution)/shard_map/ppermute | solution.py:704
  77.5 2.0 %collective-permute-done.10.refs_2_ = bf16[352,768]{1,0:T(8,128)(2,1)S(1)} collective-permute-done((bf16[352,768]{1,0:T(8,128)(2,1)S(1)}, bf16[352,768]{1,0:T(8,128)(2,1)S(1)}, u32[]{:S(2)}, u32[]{:S(2)}) %collective-permute-start.10) | collective-permute-done | bytes 540704 | tf_op jit(solution)/shard_map/ppermute | solution.py:705
  79.5 10.8 %collective-permute-done.11.refs_3_ = bf16[352,768]{1,0:T(8,128)(2,1)S(1)} collective-permute-done((bf16[352,768]{1,0:T(8,128)(2,1)S(1)}, bf16[352,768]{1,0:T(8,128)(2,1)S(1)}, u32[]{:S(2)}, u32[]{:S(2)}) %collective-permute-start.11) | collective-permute-done | bytes 540704 | tf_op jit(solution)/shard_map/ppermute | solution.py:706
  91.4 0.9 collective-permute-done.14.refs_9_
  92.3 2.3 %shard_map.155 = (bf16[3,768,768]{2,1,0:T(8,128)(2,1)S(1)}, bf16[3,768,768]{2,1,0:T(8,128)(2,1)S(1)}, f32[4,768]{1,0:T(4,128)S(1)}) custom-call(s32[4]{0:T(128)S(1)} %copy-done.10, f32[1,768]{1,0:T(1,128)S(1)} %copy-done.9, bf16[1,768,768]{2,1,0:T(8,128)(2,1)S(1)} %copy-done, bf16[1,768,768]{2,1,0:T(8,128)(2,1)S(1)} %copy-done.2, ...), custom_call_target="tpu_custom_call" | custom-call | flops 100000000 | bytes 300000 | tf_op jit(solution)/shard_map/pallas_call | solution.py:184
  94.6 6.5 %shard_map.156 = (bf16[352,384]{1,0:T(8,128)(2,1)S(1)}, bf16[352,384]{1,0:T(8,128)(2,1)S(1)}, bf16[352,384]{1,0:T(8,128)(2,1)S(1)}, bf16[352,384]{1,0:T(8,128)(2,1)S(1)}) custom-call(s32[4]{0:T(128)S(1)} %copy-done.10, s32[1]{0:T(128)} %get-tuple-element.42.refs_1_, bf16[352,768]{1,0:T(8,128)(2,1)S(1)} %get-tuple-element.63.refs_2_, ...), custom_call_target="tpu_custom_call" | custom-call | flops 8999999488 | bytes 27000000 | tf_op jit(solution)/shard_map/pallas_call | solution.py:184
  101.1 1.6 %collective-permute-start.18 = (bf16[352,384]{1,0:T(8,128)(2,1)S(1)}, bf16[352,384]{1,0:T(8,128)(2,1)S(1)}, u32[]{:S(2)}, u32[]{:S(2)}) collective-permute-start(bf16[352,384]{1,0:T(8,128)(2,1)S(1)} %get-tuple-element.74), channel_id=1, source_target_pairs={{0,2},{2,0},{1,3},{3,1},{4,6},{6,4},{5,7},{7,5},{8,10},{10,8},{9,1... | collective-permute-start | bytes 811016 | tf_op jit(solution)/shard_map/ppermute | solution.py:744
  102.7 1.6 %collective-permute-start.19 = (bf16[352,384]{1,0:T(8,128)(2,1)S(1)}, bf16[352,384]{1,0:T(8,128)(2,1)S(1)}, u32[]{:S(2)}, u32[]{:S(2)}) collective-permute-start(bf16[352,384]{1,0:T(8,128)(2,1)S(1)} %get-tuple-element.75), channel_id=1, source_target_pairs={{0,4},{4,0},{8,12},{12,8},{1,5},{5,1},{9,13},{13,9},{2,6},{6,2},{1... | collective-permute-start | bytes 811016 | tf_op jit(solution)/shard_map/ppermute | solution.py:742
  104.7 5.0 %collective-permute-done.18.refs_2_ = bf16[352,384]{1,0:T(8,128)(2,1)S(1)} collective-permute-done((bf16[352,384]{1,0:T(8,128)(2,1)S(1)}, bf16[352,384]{1,0:T(8,128)(2,1)S(1)}, u32[]{:S(2)}, u32[]{:S(2)}) %collective-permute-start.18) | collective-permute-done | bytes 270368 | tf_op jit(solution)/shard_map/ppermute | solution.py:744
  109.7 2.3 %collective-permute-done.19.refs_3_ = bf16[352,384]{1,0:T(8,128)(2,1)S(1)} collective-permute-done((bf16[352,384]{1,0:T(8,128)(2,1)S(1)}, bf16[352,384]{1,0:T(8,128)(2,1)S(1)}, u32[]{:S(2)}, u32[]{:S(2)}) %collective-permute-start.19) | collective-permute-done | bytes 270368 | tf_op jit(solution)/shard_map/ppermute | solution.py:742
  112.0 4.6 %collective-permute-done.20.refs_4_ = bf16[352,384]{1,0:T(8,128)(2,1)S(1)} collective-permute-done((bf16[352,384]{1,0:T(8,128)(2,1)S(1)}, bf16[352,384]{1,0:T(8,128)(2,1)S(1)}, u32[]{:S(2)}, u32[]{:S(2)}) %collective-permute-start.20) | collective-permute-done | bytes 270368 | tf_op jit(solution)/shard_map/ppermute | solution.py:743
  116.7 3.1 %shard_map.157 = bf16[1024,384]{1,0:T(8,128)(2,1)} custom-call(s32[1024,128]{1,0:T(8,128)S(1)} %get-tuple-element.41.refs_0_, bf16[352,384]{1,0:T(8,128)(2,1)S(1)} %get-tuple-element.73.refs_1_, bf16[352,384]{1,0:T(8,128)(2,1)S(1)} %collective-permute-done.18.refs_2_, bf16[352,384]{1,0:T(8,128)(2,1)S(1)} %collective-permute-done.19.refs_3_, ...), custom_call_target="tpu_custom_call" | custom-call | flops 1000000000 | bytes 3000000 | tf_op jit(solution)/shard_map/pallas_call | solution.py:184
  (56 shorter events, 4.0 us)
Async XLA Ops:
  3.2 37.9 %collective-permute-start.4 = (bf16[400,768]{1,0:T(8,128)(2,1)}, bf16[400,768]{1,0:T(8,128)(2,1)S(1)}, u32[]{:S(2)}, u32[]{:S(2)}) collective-permute-start(bf16[400,768]{1,0:T(8,128)(2,1)} %shard_map.146.refs_6_), channel_id=1, source_target_pairs={{0,8},{4,12},{8,0},{12,4},{1,9},{5,13},{9,1},{13,5},{2,10},{6,14},... | collective-permute-start | bytes 1843208 | tf_op jit(solution)/shard_map/ppermute | solution.py:582
  7.3 9.7 %copy-start = (bf16[1,768,768]{2,1,0:T(8,128)(2,1)S(1)}, bf16[1,768,768]{2,1,0:T(8,128)(2,1)}, u32[]{:S(2)}) copy-start(bf16[1,768,768]{2,1,0:T(8,128)(2,1)} %refs_2_.9) | copy-start | bytes 3538948
  7.3 9.7 %copy-start.9 = (f32[1,768]{1,0:T(1,128)S(1)}, f32[1,768]{1,0:T(1,128)}, u32[]{:S(2)}) copy-start(f32[1,768]{1,0:T(1,128)} %refs_1_.11) | copy-start | bytes 9220
  7.3 9.7 %copy-start.10 = (s32[4]{0:T(128)S(1)}, s32[4]{0:T(128)}, u32[]{:S(2)}) copy-start(s32[4]{0:T(128)} %pad_add_fusion.refs_0_) | copy-start | bytes 52
  19.2 2.4 %copy-start.14 = (s32[1024]{0:T(1024)S(1)}, s32[1024]{0:T(1024)}, u32[]{:S(2)}) copy-start(s32[1024]{0:T(1024)} %param.25) | copy-start | bytes 12292
  19.2 2.4 %copy-start.15 = (s32[16]{0:T(128)S(1)}, s32[16]{0:T(128)}, u32[]{:S(2)}) copy-start(s32[16]{0:T(128)} %refs_1_.6) | copy-start | bytes 196
  19.2 11.8 %copy-start.3 = (bf16[1024,768]{1,0:T(8,128)(2,1)S(1)}, bf16[1024,768]{1,0:T(8,128)(2,1)}, u32[]{:S(2)}) copy-start(bf16[1024,768]{1,0:T(8,128)(2,1)} %refs_0_.3) | copy-start | bytes 4718596
  19.2 11.8 %copy-start.5 = (bf16[768,768]{1,0:T(8,128)(2,1)S(1)}, bf16[768,768]{1,0:T(8,128)(2,1)}, u32[]{:S(2)}) copy-start(bf16[768,768]{1,0:T(8,128)(2,1)} %refs_1_.9) | copy-start | bytes 3538948
  20.1 42.7 %collective-permute-start.8 = (bf16[784,768]{1,0:T(8,128)(2,1)S(1)}, bf16[784,768]{1,0:T(8,128)(2,1)S(1)}, u32[]{:S(2)}, u32[]{:S(2)}) collective-permute-start(bf16[784,768]{1,0:T(8,128)(2,1)S(1)} %shard_map.153), channel_id=1, source_target_pairs={{0,2},{2,0},{1,3},{3,1},{4,6},{6,4},{5,7},{7,5},{8,10},{10,8},{9,1... | collective-permute-start | bytes 3612680 | tf_op jit(solution)/shard_map/ppermute | solution.py:625
  21.7 1.7 %collective-permute-start = (bf16[144,768]{1,0:T(8,128)(2,1)S(1)}, bf16[144,768]{1,0:T(8,128)(2,1)S(1)}, u32[]{:S(2)}, u32[]{:S(2)}) collective-permute-start(bf16[144,768]{1,0:T(8,128)(2,1)S(1)} %copy-done.6), channel_id=1, source_target_pairs={{0,1},{1,0},{2,3},{3,2},{4,5},{5,4},{6,7},{7,6},{8,9},{9,8},{10,11... | collective-permute-start | bytes 663560 | tf_op jit(solution)/shard_map/ppermute | solution.py:612
  24.0 17.0 %collective-permute-start.1 = (bf16[144,384]{1,0:T(8,128)(2,1)S(1)}, bf16[144,384]{1,0:T(8,128)(2,1)S(1)}, u32[]{:S(2)}, u32[]{:S(2)}) collective-permute-start(bf16[144,384]{1,0:T(8,128)(2,1)S(1)} %shard_map.148.refs_2_), channel_id=1, source_target_pairs={{0,4},{4,8},{8,12},{1,5},{5,9},{9,13},{2,6},{6,10},{10,14},{3,7},{... | collective-permute-start | bytes 331784 | tf_op jit(solution)/shard_map/ppermute | solution.py:621
  27.5 13.5 %collective-permute-start.2 = (bf16[144,384]{1,0:T(8,128)(2,1)S(1)}, bf16[144,384]{1,0:T(8,128)(2,1)S(1)}, u32[]{:S(2)}, u32[]{:S(2)}) collective-permute-start(bf16[144,384]{1,0:T(8,128)(2,1)S(1)} %shard_map.148.refs_2_), channel_id=1, source_target_pairs={{0,8},{4,12},{1,9},{5,13},{2,10},{6,14},{3,11},{7,15},{16,24},{20,... | collective-permute-start | bytes 331784 | tf_op jit(solution)/shard_map/ppermute | solution.py:621
  29.7 11.3 %collective-permute-start.3 = (bf16[144,384]{1,0:T(8,128)(2,1)S(1)}, bf16[144,384]{1,0:T(8,128)(2,1)S(1)}, u32[]{:S(2)}, u32[]{:S(2)}) collective-permute-start(bf16[144,384]{1,0:T(8,128)(2,1)S(1)} %shard_map.148.refs_2_), channel_id=1, source_target_pairs={{0,12},{1,13},{2,14},{3,15},{16,28},{17,29},{18,30},{19,31}} | collective-permute-start | bytes 331784 | tf_op jit(solution)/shard_map/ppermute | solution.py:621
  41.0 3.6 %copy-start.4 = (bf16[768,768]{1,0:T(8,128)(2,1)S(1)}, bf16[768,768]{1,0:T(8,128)(2,1)}, u32[]{:S(2)}) copy-start(bf16[768,768]{1,0:T(8,128)(2,1)} %refs_9_.1) | copy-start | bytes 3538948
  41.0 3.6 %copy-start.11 = (f32[768]{0:T(1024)S(1)}, f32[768]{0:T(1024)}, u32[]{:S(2)}) copy-start(f32[768]{0:T(1024)} %refs_8_.1) | copy-start | bytes 9220
  41.1 20.1 %collective-permute-start.6 = (bf16[400,768]{1,0:T(8,128)(2,1)S(1)}, bf16[400,768]{1,0:T(8,128)(2,1)S(1)}, u32[]{:S(2)}, u32[]{:S(2)}) collective-permute-start(bf16[400,768]{1,0:T(8,128)(2,1)S(1)} %collective-permute-done.4.refs_5_.refs_6_), channel_id=1, source_target_pairs={{0,2},{2,0},{1,3},{3,1},{4,6},{6,4},{5,7},{7,5},{8,10},{10,8},{9,1... | collective-permute-start | bytes 1843208 | tf_op jit(solution)/shard_map/ppermute | solution.py:671
  41.8 21.0 %collective-permute-start.7 = (bf16[400,768]{1,0:T(8,128)(2,1)S(1)}, bf16[400,768]{1,0:T(8,128)(2,1)S(1)}, u32[]{:S(2)}, u32[]{:S(2)}) collective-permute-start(bf16[400,768]{1,0:T(8,128)(2,1)S(1)} %collective-permute-done.4.refs_5_.refs_6_), channel_id=1, source_target_pairs={{0,16},{16,0},{1,17},{17,1},{2,18},{18,2},{3,19},{19,3},{4,20},{20... | collective-permute-start | bytes 1843208 | tf_op jit(solution)/shard_map/ppermute | solution.py:672
  43.3 1.3 %collective-permute-start.5 = (bf16[128,384]{1,0:T(8,128)(2,1)S(1)}, bf16[128,384]{1,0:T(8,128)(2,1)S(1)}, u32[]{:S(2)}, u32[]{:S(2)}) collective-permute-start(bf16[128,384]{1,0:T(8,128)(2,1)S(1)} %shard_map.151.refs_5_), channel_id=1, source_target_pairs={{0,1},{1,0},{2,3},{3,2},{4,5},{5,4},{6,7},{7,6},{8,9},{9,8},{10,11... | collective-permute-start | bytes 294920 | tf_op jit(solution)/shard_map/ppermute | solution.py:673
  44.6 45.7 %copy-start.12 = (f32[768]{0:T(1024)S(1)}, f32[768]{0:T(1024)}, u32[]{:S(2)}) copy-start(f32[768]{0:T(1024)} %refs_4_.1) | copy-start | bytes 9220
  53.7 38.7 %copy-start.2 = (bf16[1,768,768]{2,1,0:T(8,128)(2,1)S(1)}, bf16[1,768,768]{2,1,0:T(8,128)(2,1)}, u32[]{:S(2)}) copy-start(bf16[1,768,768]{2,1,0:T(8,128)(2,1)} %refs_3_.5) | copy-start | bytes 3538948
  61.3 29.6 %collective-permute-start.15 = (bf16[400,768]{1,0:T(8,128)(2,1)S(1)}, bf16[400,768]{1,0:T(8,128)(2,1)S(1)}, u32[]{:S(2)}, u32[]{:S(2)}) collective-permute-start(bf16[400,768]{1,0:T(8,128)(2,1)S(1)} %collective-permute-done.6.refs_7_), channel_id=1, source_target_pairs={{0,16},{16,0},{1,17},{17,1},{2,18},{18,2},{3,19},{19,3},{4,20},{20... | collective-permute-start | bytes 1843208 | tf_op jit(solution)/shard_map/ppermute | solution.py:709
  62.8 29.5 %collective-permute-start.12 = (bf16[784,768]{1,0:T(8,128)(2,1)S(1)}, bf16[784,768]{1,0:T(8,128)(2,1)S(1)}, u32[]{:S(2)}, u32[]{:S(2)}) collective-permute-start(bf16[784,768]{1,0:T(8,128)(2,1)S(1)} %collective-permute-done.8.refs_4_), channel_id=1, source_target_pairs={{0,1},{1,0},{2,3},{3,2},{4,5},{5,4},{6,7},{7,6},{8,9},{9,8},{10,11... | collective-permute-start | bytes 3612680 | tf_op jit(solution)/shard_map/ppermute | solution.py:717
  62.8 14.7 %collective-permute-start.9 = (bf16[352,768]{1,0:T(8,128)(2,1)S(1)}, bf16[352,768]{1,0:T(8,128)(2,1)S(1)}, u32[]{:S(2)}, u32[]{:S(2)}) collective-permute-start(bf16[352,768]{1,0:T(8,128)(2,1)S(1)} %get-tuple-element.54), channel_id=1, source_target_pairs={{0,2},{2,0},{1,3},{3,1},{4,6},{6,4},{5,7},{7,5},{8,10},{10,8},{9,1... | collective-permute-start | bytes 1622024 | tf_op jit(solution)/shard_map/ppermute | solution.py:704
  64.4 15.1 %collective-permute-start.10 = (bf16[352,768]{1,0:T(8,128)(2,1)S(1)}, bf16[352,768]{1,0:T(8,128)(2,1)S(1)}, u32[]{:S(2)}, u32[]{:S(2)}) collective-permute-start(bf16[352,768]{1,0:T(8,128)(2,1)S(1)} %get-tuple-element.58), channel_id=1, source_target_pairs={{0,4},{4,0},{8,12},{12,8},{1,5},{5,1},{9,13},{13,9},{2,6},{6,2},{1... | collective-permute-start | bytes 1622024 | tf_op jit(solution)/shard_map/ppermute | solution.py:705
  65.9 24.3 %collective-permute-start.11 = (bf16[352,768]{1,0:T(8,128)(2,1)S(1)}, bf16[352,768]{1,0:T(8,128)(2,1)S(1)}, u32[]{:S(2)}, u32[]{:S(2)}) collective-permute-start(bf16[352,768]{1,0:T(8,128)(2,1)S(1)} %get-tuple-element.62), channel_id=1, source_target_pairs={{0,6},{2,4},{4,2},{6,0},{8,14},{10,12},{12,10},{14,8},{1,7},{3,5},... | collective-permute-start | bytes 1622024 | tf_op jit(solution)/shard_map/ppermute | solution.py:706
  77.5 13.9 %collective-permute-start.13 = (bf16[400,768]{1,0:T(8,128)(2,1)S(1)}, bf16[400,768]{1,0:T(8,128)(2,1)S(1)}, u32[]{:S(2)}, u32[]{:S(2)}) collective-permute-start(bf16[400,768]{1,0:T(8,128)(2,1)S(1)} %collective-permute-done.4.refs_5_.refs_6_), channel_id=1, source_target_pairs={{0,1},{1,0},{2,3},{3,2},{4,5},{5,4},{6,7},{7,6},{8,9},{9,8},{10,11... | collective-permute-start | bytes 1843208 | tf_op jit(solution)/shard_map/ppermute | solution.py:717
  79.5 15.1 %collective-permute-start.16 = (bf16[400,768]{1,0:T(8,128)(2,1)S(1)}, bf16[400,768]{1,0:T(8,128)(2,1)S(1)}, u32[]{:S(2)}, u32[]{:S(2)}) collective-permute-start(bf16[400,768]{1,0:T(8,128)(2,1)S(1)} %collective-permute-done.6.refs_7_), channel_id=1, source_target_pairs={{0,1},{1,0},{2,3},{3,2},{4,5},{5,4},{6,7},{7,6},{8,9},{9,8},{10,11... | collective-permute-start | bytes 1843208 | tf_op jit(solution)/shard_map/ppermute | solution.py:717
  90.3 2.0 %collective-permute-start.14 = (bf16[400,768]{1,0:T(8,128)(2,1)S(1)}, bf16[400,768]{1,0:T(8,128)(2,1)S(1)}, u32[]{:S(2)}, u32[]{:S(2)}) collective-permute-start(bf16[400,768]{1,0:T(8,128)(2,1)S(1)} %collective-permute-done.7.refs_7_), channel_id=1, source_target_pairs={{0,1},{1,0},{2,3},{3,2},{4,5},{5,4},{6,7},{7,6},{8,9},{9,8},{10,11... | collective-permute-start | bytes 1843208 | tf_op jit(solution)/shard_map/ppermute | solution.py:717
  90.8 3.8 %collective-permute-start.17 = (bf16[400,768]{1,0:T(8,128)(2,1)S(1)}, bf16[400,768]{1,0:T(8,128)(2,1)S(1)}, u32[]{:S(2)}, u32[]{:S(2)}) collective-permute-start(bf16[400,768]{1,0:T(8,128)(2,1)S(1)} %collective-permute-done.15.refs_8_), channel_id=1, source_target_pairs={{0,1},{1,0},{2,3},{3,2},{4,5},{5,4},{6,7},{7,6},{8,9},{9,8},{10,11... | collective-permute-start | bytes 1843208 | tf_op jit(solution)/shard_map/ppermute | solution.py:718
  101.1 8.6 %collective-permute-start.18 = (bf16[352,384]{1,0:T(8,128)(2,1)S(1)}, bf16[352,384]{1,0:T(8,128)(2,1)S(1)}, u32[]{:S(2)}, u32[]{:S(2)}) collective-permute-start(bf16[352,384]{1,0:T(8,128)(2,1)S(1)} %get-tuple-element.74), channel_id=1, source_target_pairs={{0,2},{2,0},{1,3},{3,1},{4,6},{6,4},{5,7},{7,5},{8,10},{10,8},{9,1... | collective-permute-start | bytes 811016 | tf_op jit(solution)/shard_map/ppermute | solution.py:744
  102.7 9.4 %collective-permute-start.19 = (bf16[352,384]{1,0:T(8,128)(2,1)S(1)}, bf16[352,384]{1,0:T(8,128)(2,1)S(1)}, u32[]{:S(2)}, u32[]{:S(2)}) collective-permute-start(bf16[352,384]{1,0:T(8,128)(2,1)S(1)} %get-tuple-element.75), channel_id=1, source_target_pairs={{0,4},{4,0},{8,12},{12,8},{1,5},{5,1},{9,13},{13,9},{2,6},{6,2},{1... | collective-permute-start | bytes 811016 | tf_op jit(solution)/shard_map/ppermute | solution.py:742
  104.2 12.4 %collective-permute-start.20 = (bf16[352,384]{1,0:T(8,128)(2,1)S(1)}, bf16[352,384]{1,0:T(8,128)(2,1)S(1)}, u32[]{:S(2)}, u32[]{:S(2)}) collective-permute-start(bf16[352,384]{1,0:T(8,128)(2,1)S(1)} %get-tuple-element.76), channel_id=1, source_target_pairs={{0,6},{2,4},{4,2},{6,0},{8,14},{10,12},{12,10},{14,8},{1,7},{3,5},... | collective-permute-start | bytes 811016 | tf_op jit(solution)/shard_map/ppermute | solution.py:743
  (5 other events, 9.2 us)

commit v2 on v1

--- a/solution.py
+++ b/solution.py
@@ -212,7 +212,7 @@
 
 
 def spread_heads(v, lanes):
-    return sum(dot(part, lanes) for part in split(v, 2))
+    return dot(jnp.concatenate(split(v, 2), axis=1), jnp.concatenate([lanes, lanes], axis=0))
 
 
 def iota(shape, dim):
@@ -371,7 +371,7 @@
     return (total * lax.rsqrt(mean + 1e-05) * gain[...][None, :]).astype(BF16)
 
 
-def mix_kernel(keep, recv, term_1, term_2, gain, away, local):
+def mix_kernel(term_1, recv, term_2, keep, gain, away, local):
     away[...] = mixed(term_1, term_2, gain)
     local[...] = mixed(keep, recv, gain)
 
@@ -570,7 +570,7 @@
         return call(
             payload_kernel,
             arr((2 * rows + TILE, width), BF16),
-            micros=0.1,
+            micros=0.001,
             room=room,
             in_specs=[SMEM, VMEM, ANY, ANY],
             out_specs=VMEM,
@@ -592,7 +592,7 @@
         ),
         room=62,
         after=(share,),
-        micros=0.1,
+        micros=0.001,
         grid=grid,
         in_specs=[
             hold((rows, width), lambda i: (i, 0)),
@@ -613,7 +613,7 @@
     chip = call(
         chip_kernel,
         arr((nstate + TILE, channels // 2), BF16),
-        micros=0.1,
+        micros=0.001,
         in_specs=[SMEM, VMEM, VMEM],
         out_specs=VMEM,
     )(info, summary, beside)
@@ -626,7 +626,7 @@
     slot, column, flag = call(
         lambda *refs: route_kernel(cold, *refs),
         (arr((1, length), jnp.int32), arr((length, 128), jnp.int32), arr((1,), jnp.int32)),
-        micros=0.1,
+        micros=0.001,
         in_specs=[SMEM, SMEM, VMEM],
         out_specs=(VMEM, VMEM, SMEM),
     )(info, port_shard, port[None, :])
@@ -634,7 +634,7 @@
         gate_kernel,
         arr((length, channels), F32),
         room=24,
-        micros=0.1,
+        micros=0.001,
         grid=grid,
         in_specs=[hold((rows, width), lambda i: (i, 0)), fixed(w_gate.shape)],
         out_specs=hold((rows, channels), lambda i: (i, 0)),
@@ -644,7 +644,7 @@
         within_kernel,
         (arr((length, channels), F32), arr((length, heads), F32)),
         room=24,
-        micros=2.0,
+        micros=0.001,
         grid=(length // SPAN,),
         in_specs=[
             hold((SPAN, channels), lambda i: (i, 0)),
@@ -662,7 +662,7 @@
     carry = call(
         carry_kernel,
         arr((nstate, channels // 2), BF16),
-        micros=0.1,
+        micros=0.001,
         in_specs=[VMEM] * len(earlier),
         out_specs=VMEM,
         after=(past, slot, far),
@@ -672,18 +672,19 @@
     far_y = lax.ppermute(far, "groups", swap)
     carry_beside = lax.ppermute(carry, "sub", swap)
 
+    wide = 2 * rows
     blocks = call(
         norm_kernel,
         (arr((count, width), BF16),) * 4,
         room=24,
-        micros=0.1,
-        grid=grid,
+        micros=0.001,
+        grid=(length // wide,),
         in_specs=[
             SMEM,
-            hold((rows, channels), lambda i: (i, 0)),
-            hold((rows, channels), lambda i: (i, 0)),
-            hold((rows, 2 * nstate), lambda i: (i, 0)),
-            hold((rows, heads), lambda i: (i, 0)),
+            hold((wide, channels), lambda i: (i, 0)),
+            hold((wide, channels), lambda i: (i, 0)),
+            hold((wide, 2 * nstate), lambda i: (i, 0)),
+            hold((wide, heads), lambda i: (i, 0)),
             fixed(carry.shape),
             fixed(carry.shape),
             fixed(beside.shape),
@@ -697,20 +698,18 @@
     near = [(i, i ^ 1) for i in range(shard_count)]
     near_x = [(2 * i + j, 2 * (i ^ 1) + (j ^ 1)) for i in range(shard_count) for j in range(2)]
     keep, beside_rows, same, other = blocks
-    for piece in (far_x, far_y, own):
-        beside_rows, same, other = (tie(a, piece) for a in (beside_rows, same, other))
     terms = (
+        lax.ppermute(same, "tm", near),
+        lax.ppermute(beside_rows, "mp", swap),
+        lax.ppermute(other, ("tm", "mp"), near_x),
         keep,
-        lax.ppermute(beside_rows, "mp", swap),
-        lax.ppermute(same, "tm", near),
-        lax.ppermute(other, ("tm", "mp"), near_x),
     )
     own, far, far_y, far_x = (tie(a, keep) for a in (own, far, far_y, far_x))
     far_xy = lax.ppermute(far_x, "groups", swap)
     away, local = call(
         mix_kernel,
         (arr((count, width), BF16),) * 2,
-        micros=0.1,
+        micros=5,
         in_specs=[VMEM] * 5,
         out_specs=(VMEM,) * 2,
     )(*terms, mix_gain)
@@ -747,9 +746,9 @@
         collect_kernel,
         arr((length, side), BF16),
         micros=1,
-        grid=grid,
-        in_specs=[hold((rows, 128), lambda i: (i, 0))] + [fixed((count, side))] * 4,
-        out_specs=hold((rows, side), lambda i: (i, 0)),
+        grid=(length // (2 * rows),),
+        in_specs=[hold((2 * rows, 128), lambda i: (i, 0))] + [fixed((count, side))] * 4,
+        out_specs=hold((2 * rows, side), lambda i: (i, 0)),
         scratch_shapes=[pltpu.VMEM((4 * count, side), BF16)],
     )(column, same_l, back_l, back_same, back_other)
 

time: 120 us -> 115 us (0.958)
  waiting for transfers between devices: 45.7 us -> 38.5 us
  starting transfers between devices: 24 us -> 28.8 us
  Pallas kernels: 46.8 us -> 44.2 us
    ppermute x1, waiting for transfers between devices: 10.8 us -> 0.01 us  [fast(): lax.ppermute(other, ('tm', 'mp'), near_x)]
    ppermute x1, waiting for transfers between devices: 11.1 us -> 14.9 us  [fast(): lax.ppermute(beside_rows, 'mp', swap)]
    ppermute x1, starting transfers between devices: 1.57 us -> 5.26 us  [fast(): lax.ppermute(same, 'tm', near)]
    ppermute x1, waiting for transfers between devices: 7.61 us -> 4.71 us  [fast(): far_x = lax.ppermute(far, 'mp', swap)]
    pallas_call x13, Pallas kernels: 46.8 us -> 44.2 us  [call(): return lambda *args: run(*args, *after)]
    ppermute x1, starting transfers between devices: 0.42 us -> 2.5 us  [fast(): lax.ppermute(other, ('tm', 'mp'), near_x)]
    ppermute x1, waiting for transfers between devices: 1.99 us -> 3.79 us  [fast(): lax.ppermute(same, 'tm', near)]
  transfers between devices with their start and end apart: 21 -> 21, of which waited for: 9 -> 8; matrix products, arithmetic and copies ran while one was open for 0% -> 0% of each run, Pallas kernels for 29% -> 28%
where the time goes in v2:
time: 115 us
  Pallas kernels  44.2 us (38%)
  waiting for transfers between devices  38.5 us (33%)
  starting transfers between devices  28.8 us (25%)
  local copies, waits for them, and re-layouts  2.26 us (2%)
    pallas_call x13, Pallas kernels, call(): return lambda *args: run(*args, *after)  44.2 us
    ppermute x1, waiting for transfers between devices, fast(): lax.ppermute(beside_rows, 'mp', swap)  14.9 us
    ppermute x3, starting transfers between devices, fast(): lax.ppermute(chip, 'tm', [(i, i + hop) for i in range(shard_count - hop)])  7.03 us
    ppermute x1, starting transfers between devices, fast(): lax.ppermute(same, 'tm', near)  5.26 us
    ppermute x1, waiting for transfers between devices, fast(): back_l = lax.ppermute(other_l, 'mp', swap)  5.03 us
    ppermute x1, waiting for transfers between devices, fast(): far_x = lax.ppermute(far, 'mp', swap)  4.71 us
    ppermute x1, waiting for transfers between devices, fast(): back_other = lax.ppermute(other, ('tm', 'mp'), near_x)  4.64 us
    ppermute x1, starting transfers between devices, fast(): far = lax.ppermute(share, 'tm', [(i, i ^ 2) for i in range(shard_count)])  4.1 us
  transfers between devices with their start and end apart: 21, of which 8 were waited for; matrix products, arithmetic and copies ran while one was open for 0% of the time, Pallas kernels for 28%

profile of v2, /device:TPU:0, one launch (start us, length us, event | category | flops | bytes accessed | tf_op | source)
XLA Modules:
  0.0 114.7 jit_solution(13652896623057583138)
XLA Ops:
  0.6 2.6 %shard_map.146.refs_6_ = bf16[400,768]{1,0:T(8,128)(2,1)} custom-call(s32[4]{0:T(128)} %pad_add_fusion.refs_0_, f32[1,768]{1,0:T(1,128)} %refs_1_.11, bf16[1,768,768]{2,1,0:T(8,128)(2,1)} %refs_2_.9, bf16[1,768,768]{2,1,0:T(8,128)(2,1)} %refs_3_.5), custom_call_target="tpu_custom_call" | custom-call | flops 1000000 | bytes 3000 | tf_op jit(solution)/shard_map/pallas_call | solution.py:184
  3.2 4.1 %collective-permute-start.4 = (bf16[400,768]{1,0:T(8,128)(2,1)}, bf16[400,768]{1,0:T(8,128)(2,1)S(1)}, u32[]{:S(2)}, u32[]{:S(2)}) collective-permute-start(bf16[400,768]{1,0:T(8,128)(2,1)} %shard_map.146.refs_6_), channel_id=1, source_target_pairs={{0,8},{4,12},{8,0},{12,4},{1,9},{5,13},{9,1},{13,5},{2,10},{6,14},... | collective-permute-start | bytes 1843208 | tf_op jit(solution)/shard_map/ppermute | solution.py:582
  7.3 8.9 %shard_map.147 = (bf16[1024,768]{1,0:T(8,128)(2,1)}, bf16[1024,256]{1,0:T(8,128)(2,1)}, bf16[144,768]{1,0:T(8,128)(2,1)}) custom-call(bf16[1024,768]{1,0:T(8,128)(2,1)} %refs_0_.3, bf16[768,768]{1,0:T(8,128)(2,1)} %refs_1_.8, bf16[768,256]{1,0:T(8,128)(2,1)} %refs_2_.6, bf16[12,768]{1,0:T(8,128)(2,1)} %bitcast.8, f32[1,12]{1,0:T(1,128)} %bitcast.9, ...), custom_call_target="tpu_custom_call" | custom-call | flops 1000000 | bytes 3000 | tf_op jit(solution)/shard_map/pallas_call | solution.py:184
  16.3 1.3 %copy-done.1 = bf16[1,768,768]{2,1,0:T(8,128)(2,1)S(1)} copy-done((bf16[1,768,768]{2,1,0:T(8,128)(2,1)S(1)}, bf16[1,768,768]{2,1,0:T(8,128)(2,1)}, u32[]{:S(2)}) %copy-start.1) | copy-done | bytes 1179672
  17.6 0.9 copy-done.8
  18.5 0.8 shard_map.154
  19.4 1.6 %collective-permute-start.9 = (bf16[784,768]{1,0:T(8,128)(2,1)S(1)}, bf16[784,768]{1,0:T(8,128)(2,1)S(1)}, u32[]{:S(2)}, u32[]{:S(2)}) collective-permute-start(bf16[784,768]{1,0:T(8,128)(2,1)S(1)} %shard_map.154), channel_id=1, source_target_pairs={{0,2},{2,0},{1,3},{3,1},{4,6},{6,4},{5,7},{7,5},{8,10},{10,8},{9,1... | collective-permute-start | bytes 3612680 | tf_op jit(solution)/shard_map/ppermute | solution.py:625
  20.9 0.6 shard_map.148.refs_2_
  21.5 3.5 %collective-permute-start.1 = (bf16[144,384]{1,0:T(8,128)(2,1)S(1)}, bf16[144,384]{1,0:T(8,128)(2,1)S(1)}, u32[]{:S(2)}, u32[]{:S(2)}) collective-permute-start(bf16[144,384]{1,0:T(8,128)(2,1)S(1)} %shard_map.148.refs_2_), channel_id=1, source_target_pairs={{0,4},{4,8},{8,12},{1,5},{5,9},{9,13},{2,6},{6,10},{10,14},{3,7},{... | collective-permute-start | bytes 331784 | tf_op jit(solution)/shard_map/ppermute | solution.py:621
  25.0 2.2 %collective-permute-start.2 = (bf16[144,384]{1,0:T(8,128)(2,1)S(1)}, bf16[144,384]{1,0:T(8,128)(2,1)S(1)}, u32[]{:S(2)}, u32[]{:S(2)}) collective-permute-start(bf16[144,384]{1,0:T(8,128)(2,1)S(1)} %shard_map.148.refs_2_), channel_id=1, source_target_pairs={{0,8},{4,12},{1,9},{5,13},{2,10},{6,14},{3,11},{7,15},{16,24},{20,... | collective-permute-start | bytes 331784 | tf_op jit(solution)/shard_map/ppermute | solution.py:621
  27.3 1.3 %collective-permute-start.3 = (bf16[144,384]{1,0:T(8,128)(2,1)S(1)}, bf16[144,384]{1,0:T(8,128)(2,1)S(1)}, u32[]{:S(2)}, u32[]{:S(2)}) collective-permute-start(bf16[144,384]{1,0:T(8,128)(2,1)S(1)} %shard_map.148.refs_2_), channel_id=1, source_target_pairs={{0,12},{1,13},{2,14},{3,15},{16,28},{17,29},{18,30},{19,31}} | collective-permute-start | bytes 331784 | tf_op jit(solution)/shard_map/ppermute | solution.py:621
  28.6 1.7 %shard_map.145 = (s32[1,1024]{1,0:T(1,128)S(1)}, s32[1024,128]{1,0:T(8,128)S(1)}, s32[1]{0:T(128)}) custom-call(s32[4]{0:T(128)S(1)} %copy-done.11, s32[16]{0:T(128)S(1)} %copy-done.14, s32[1,1024]{1,0:T(1,128)S(1)} %bitcast.7), custom_call_target="tpu_custom_call" | custom-call | flops 1000000 | bytes 3000 | tf_op jit(solution)/shard_map/pallas_call | solution.py:184
  30.4 2.3 %shard_map.149.refs_3_.refs_2_ = f32[1024,768]{1,0:T(8,128)S(1)} custom-call(bf16[1024,768]{1,0:T(8,128)(2,1)S(1)} %copy-done.3, bf16[768,768]{1,0:T(8,128)(2,1)S(1)} %copy-done.7, bf16[144,384]{1,0:T(8,128)(2,1)S(1)} %shard_map.148.refs_2_, s32[1,1024]{1,0:T(1,128)S(1)} %get-tuple-element.37.refs_3_.refs_4_.refs_10_), custom_call_target="tpu_custom_call" | custom-call | flops 1000000 | bytes 3000 | tf_op jit(solution)/shard_map/pallas_call | solution.py:184
  32.7 7.8 %shard_map.150 = (f32[1024,768]{1,0:T(8,128)S(1)}, f32[1024,12]{1,0:T(8,128)S(1)}) custom-call(bf16[1024,768]{1,0:T(8,128)(2,1)S(1)} %copy-done.5, bf16[1024,256]{1,0:T(8,128)(2,1)S(1)} %copy-done.4, f32[12,1024]{1,0:T(8,128)S(1)} %copy-done.9, f32[1024,768]{1,0:T(8,128)S(1)} %shard_map.149.refs_3_.refs_2_), custom_call_target="tpu_custom_call" | custom-call | flops 1000000 | bytes 3000 | tf_op jit(solution)/shard_map/pallas_call | solution.py:184
  41.2 1.5 %collective-permute-start.11 = (bf16[400,768]{1,0:T(8,128)(2,1)S(1)}, bf16[400,768]{1,0:T(8,128)(2,1)S(1)}, u32[]{:S(2)}, u32[]{:S(2)}) collective-permute-start(bf16[400,768]{1,0:T(8,128)(2,1)S(1)} %collective-permute-done.4.refs_5_.refs_6_), channel_id=1, source_target_pairs={{0,16},{16,0},{1,17},{17,1},{2,18},{18,2},{3,19},{19,3},{4,20},{20... | collective-permute-start | bytes 1843208 | tf_op jit(solution)/shard_map/ppermute | solution.py:672
  42.7 1.3 %collective-permute-done.5.refs_6_ = bf16[128,384]{1,0:T(8,128)(2,1)S(1)} collective-permute-done((bf16[128,384]{1,0:T(8,128)(2,1)S(1)}, bf16[128,384]{1,0:T(8,128)(2,1)S(1)}, u32[]{:S(2)}, u32[]{:S(2)}) %collective-permute-start.5) | collective-permute-done | bytes 98336 | tf_op jit(solution)/shard_map/ppermute | solution.py:673
  44.0 7.4 %shard_map.152 = (bf16[352,768]{1,0:T(8,128)(2,1)S(1)}, bf16[352,768]{1,0:T(8,128)(2,1)S(1)}, bf16[352,768]{1,0:T(8,128)(2,1)S(1)}, bf16[352,768]{1,0:T(8,128)(2,1)S(1)}) custom-call(s32[4]{0:T(128)S(1)} %copy-done.11, f32[1024,768]{1,0:T(8,128)S(1)} %get-tuple-element.38.refs_1_, f32[1024,768]{1,0:T(8,128)S(1)} %shard_map.149.refs_3_.refs_2_, ...), custom_call_target="tpu_custom_call" | custom-call | flops 1000000 | bytes 3000 | tf_op jit(solution)/shard_map/pallas_call | solution.py:184
  51.4 5.3 %collective-permute-start.6 = (bf16[352,768]{1,0:T(8,128)(2,1)S(1)}, bf16[352,768]{1,0:T(8,128)(2,1)S(1)}, u32[]{:S(2)}, u32[]{:S(2)}) collective-permute-start(bf16[352,768]{1,0:T(8,128)(2,1)S(1)} %get-tuple-element.40), channel_id=1, source_target_pairs={{0,4},{4,0},{8,12},{12,8},{1,5},{5,1},{9,13},{13,9},{2,6},{6,2},{1... | collective-permute-start | bytes 1622024 | tf_op jit(solution)/shard_map/ppermute | solution.py:702
  57.2 4.7 %collective-permute-done.14.refs_7_ = bf16[400,768]{1,0:T(8,128)(2,1)S(1)} collective-permute-done((bf16[400,768]{1,0:T(8,128)(2,1)S(1)}, bf16[400,768]{1,0:T(8,128)(2,1)S(1)}, u32[]{:S(2)}, u32[]{:S(2)}) %collective-permute-start.14) | collective-permute-done | bytes 614432 | tf_op jit(solution)/shard_map/ppermute | solution.py:671
  61.9 2.5 %collective-permute-start.8 = (bf16[352,768]{1,0:T(8,128)(2,1)S(1)}, bf16[352,768]{1,0:T(8,128)(2,1)S(1)}, u32[]{:S(2)}, u32[]{:S(2)}) collective-permute-start(bf16[352,768]{1,0:T(8,128)(2,1)S(1)} %get-tuple-element.42), channel_id=1, source_target_pairs={{0,6},{2,4},{4,2},{6,0},{8,14},{10,12},{12,10},{14,8},{1,7},{3,5},... | collective-permute-start | bytes 1622024 | tf_op jit(solution)/shard_map/ppermute | solution.py:704
  64.4 1.5 %collective-permute-start.15 = (bf16[400,768]{1,0:T(8,128)(2,1)S(1)}, bf16[400,768]{1,0:T(8,128)(2,1)S(1)}, u32[]{:S(2)}, u32[]{:S(2)}) collective-permute-start(bf16[400,768]{1,0:T(8,128)(2,1)S(1)} %collective-permute-done.14.refs_7_), channel_id=1, source_target_pairs={{0,16},{16,0},{1,17},{17,1},{2,18},{18,2},{3,19},{19,3},{4,20},{20... | collective-permute-start | bytes 1843208 | tf_op jit(solution)/shard_map/ppermute | solution.py:708
  65.9 3.8 %collective-permute-done.6.refs_0_ = bf16[352,768]{1,0:T(8,128)(2,1)S(1)} collective-permute-done((bf16[352,768]{1,0:T(8,128)(2,1)S(1)}, bf16[352,768]{1,0:T(8,128)(2,1)S(1)}, u32[]{:S(2)}, u32[]{:S(2)}) %collective-permute-start.6) | collective-permute-done | bytes 540704 | tf_op jit(solution)/shard_map/ppermute | solution.py:702
  69.7 14.9 %collective-permute-done.7.refs_1_ = bf16[352,768]{1,0:T(8,128)(2,1)S(1)} collective-permute-done((bf16[352,768]{1,0:T(8,128)(2,1)S(1)}, bf16[352,768]{1,0:T(8,128)(2,1)S(1)}, u32[]{:S(2)}, u32[]{:S(2)}) %collective-permute-start.7) | collective-permute-done | bytes 540704 | tf_op jit(solution)/shard_map/ppermute | solution.py:703
  85.8 1.7 %collective-permute-done.13.refs_9_ = bf16[400,768]{1,0:T(8,128)(2,1)S(1)} collective-permute-done((bf16[400,768]{1,0:T(8,128)(2,1)S(1)}, bf16[400,768]{1,0:T(8,128)(2,1)S(1)}, u32[]{:S(2)}, u32[]{:S(2)}) %collective-permute-start.13) | collective-permute-done | bytes 614432 | tf_op jit(solution)/shard_map/ppermute | solution.py:716
  87.6 2.3 %shard_map.155 = (bf16[3,768,768]{2,1,0:T(8,128)(2,1)S(1)}, bf16[3,768,768]{2,1,0:T(8,128)(2,1)S(1)}, f32[4,768]{1,0:T(4,128)S(1)}) custom-call(s32[4]{0:T(128)S(1)} %copy-done.11, f32[1,768]{1,0:T(1,128)S(1)} %copy-done.10, bf16[1,768,768]{2,1,0:T(8,128)(2,1)S(1)} %copy-done, bf16[1,768,768]{2,1,0:T(8,128)(2,1)S(1)} %copy-done.2, ...), custom_call_target="tpu_custom_call" | custom-call | flops 100000000 | bytes 300000 | tf_op jit(solution)/shard_map/pallas_call | solution.py:184
  89.9 6.5 %shard_map.156 = (bf16[352,384]{1,0:T(8,128)(2,1)S(1)}, bf16[352,384]{1,0:T(8,128)(2,1)S(1)}, bf16[352,384]{1,0:T(8,128)(2,1)S(1)}, bf16[352,384]{1,0:T(8,128)(2,1)S(1)}) custom-call(s32[4]{0:T(128)S(1)} %copy-done.11, s32[1]{0:T(128)} %get-tuple-element.33.refs_1_, bf16[352,768]{1,0:T(8,128)(2,1)S(1)} %get-tuple-element.44.refs_2_, ...), custom_call_target="tpu_custom_call" | custom-call | flops 8999999488 | bytes 27000000 | tf_op jit(solution)/shard_map/pallas_call | solution.py:184
  96.4 1.6 %collective-permute-start.18 = (bf16[352,384]{1,0:T(8,128)(2,1)S(1)}, bf16[352,384]{1,0:T(8,128)(2,1)S(1)}, u32[]{:S(2)}, u32[]{:S(2)}) collective-permute-start(bf16[352,384]{1,0:T(8,128)(2,1)S(1)} %get-tuple-element.56), channel_id=1, source_target_pairs={{0,2},{2,0},{1,3},{3,1},{4,6},{6,4},{5,7},{7,5},{8,10},{10,8},{9,1... | collective-permute-start | bytes 811016 | tf_op jit(solution)/shard_map/ppermute | solution.py:743
  97.9 1.6 %collective-permute-start.19 = (bf16[352,384]{1,0:T(8,128)(2,1)S(1)}, bf16[352,384]{1,0:T(8,128)(2,1)S(1)}, u32[]{:S(2)}, u32[]{:S(2)}) collective-permute-start(bf16[352,384]{1,0:T(8,128)(2,1)S(1)} %get-tuple-element.57), channel_id=1, source_target_pairs={{0,4},{4,0},{8,12},{12,8},{1,5},{5,1},{9,13},{13,9},{2,6},{6,2},{1... | collective-permute-start | bytes 811016 | tf_op jit(solution)/shard_map/ppermute | solution.py:741
  99.9 5.0 %collective-permute-done.18.refs_2_ = bf16[352,384]{1,0:T(8,128)(2,1)S(1)} collective-permute-done((bf16[352,384]{1,0:T(8,128)(2,1)S(1)}, bf16[352,384]{1,0:T(8,128)(2,1)S(1)}, u32[]{:S(2)}, u32[]{:S(2)}) %collective-permute-start.18) | collective-permute-done | bytes 270368 | tf_op jit(solution)/shard_map/ppermute | solution.py:743
  105.0 2.3 %collective-permute-done.19.refs_3_ = bf16[352,384]{1,0:T(8,128)(2,1)S(1)} collective-permute-done((bf16[352,384]{1,0:T(8,128)(2,1)S(1)}, bf16[352,384]{1,0:T(8,128)(2,1)S(1)}, u32[]{:S(2)}, u32[]{:S(2)}) %collective-permute-start.19) | collective-permute-done | bytes 270368 | tf_op jit(solution)/shard_map/ppermute | solution.py:741
  107.3 4.6 %collective-permute-done.20.refs_4_ = bf16[352,384]{1,0:T(8,128)(2,1)S(1)} collective-permute-done((bf16[352,384]{1,0:T(8,128)(2,1)S(1)}, bf16[352,384]{1,0:T(8,128)(2,1)S(1)}, u32[]{:S(2)}, u32[]{:S(2)}) %collective-permute-start.20) | collective-permute-done | bytes 270368 | tf_op jit(solution)/shard_map/ppermute | solution.py:742
  111.9 2.7 %shard_map.157 = bf16[1024,384]{1,0:T(8,128)(2,1)} custom-call(s32[1024,128]{1,0:T(8,128)S(1)} %get-tuple-element.32.refs_0_, bf16[352,384]{1,0:T(8,128)(2,1)S(1)} %get-tuple-element.55.refs_1_, bf16[352,384]{1,0:T(8,128)(2,1)S(1)} %collective-permute-done.18.refs_2_, bf16[352,384]{1,0:T(8,128)(2,1)S(1)} %collective-permute-done.19.refs_3_, ...), custom_call_target="tpu_custom_call" | custom-call | flops 1000000000 | bytes 3000000 | tf_op jit(solution)/shard_map/pallas_call | solution.py:184
  (56 shorter events, 3.5 us)
Async XLA Ops:
  3.2 37.3 %collective-permute-start.4 = (bf16[400,768]{1,0:T(8,128)(2,1)}, bf16[400,768]{1,0:T(8,128)(2,1)S(1)}, u32[]{:S(2)}, u32[]{:S(2)}) collective-permute-start(bf16[400,768]{1,0:T(8,128)(2,1)} %shard_map.146.refs_6_), channel_id=1, source_target_pairs={{0,8},{4,12},{8,0},{12,4},{1,9},{5,13},{9,1},{13,5},{2,10},{6,14},... | collective-permute-start | bytes 1843208 | tf_op jit(solution)/shard_map/ppermute | solution.py:582
  7.3 9.0 %copy-start = (bf16[1,768,768]{2,1,0:T(8,128)(2,1)S(1)}, bf16[1,768,768]{2,1,0:T(8,128)(2,1)}, u32[]{:S(2)}) copy-start(bf16[1,768,768]{2,1,0:T(8,128)(2,1)} %refs_2_.9) | copy-start | bytes 3538948
  7.3 9.0 %copy-start.10 = (f32[1,768]{1,0:T(1,128)S(1)}, f32[1,768]{1,0:T(1,128)}, u32[]{:S(2)}) copy-start(f32[1,768]{1,0:T(1,128)} %refs_1_.11) | copy-start | bytes 9220
  7.3 9.0 %copy-start.11 = (s32[4]{0:T(128)S(1)}, s32[4]{0:T(128)}, u32[]{:S(2)}) copy-start(s32[4]{0:T(128)} %pad_add_fusion.refs_0_) | copy-start | bytes 52
  16.2 4.7 %collective-permute-start = (bf16[144,768]{1,0:T(8,128)(2,1)}, bf16[144,768]{1,0:T(8,128)(2,1)S(1)}, u32[]{:S(2)}, u32[]{:S(2)}) collective-permute-start(bf16[144,768]{1,0:T(8,128)(2,1)} %get-tuple-element.36.refs_1_.refs_4_), channel_id=1, source_target_pairs={{0,1},{1,0},{2,3},{3,2},{4,5},{5,4},{6,7},{7,6},{8,9},{9,8},{10,11... | collective-permute-start | bytes 663560 | tf_op jit(solution)/shard_map/ppermute | solution.py:612
  18.5 10.1 %copy-start.13 = (s32[1024]{0:T(1024)S(1)}, s32[1024]{0:T(1024)}, u32[]{:S(2)}) copy-start(s32[1024]{0:T(1024)} %param.25) | copy-start | bytes 12292
  18.5 10.1 %copy-start.14 = (s32[16]{0:T(128)S(1)}, s32[16]{0:T(128)}, u32[]{:S(2)}) copy-start(s32[16]{0:T(128)} %refs_1_.6) | copy-start | bytes 196
  18.5 11.8 %copy-start.3 = (bf16[1024,768]{1,0:T(8,128)(2,1)S(1)}, bf16[1024,768]{1,0:T(8,128)(2,1)}, u32[]{:S(2)}) copy-start(bf16[1024,768]{1,0:T(8,128)(2,1)} %refs_0_.3) | copy-start | bytes 4718596
  18.5 11.8 %copy-start.7 = (bf16[768,768]{1,0:T(8,128)(2,1)S(1)}, bf16[768,768]{1,0:T(8,128)(2,1)}, u32[]{:S(2)}) copy-start(bf16[768,768]{1,0:T(8,128)(2,1)} %refs_1_.9) | copy-start | bytes 3538948
  19.4 45.0 %collective-permute-start.9 = (bf16[784,768]{1,0:T(8,128)(2,1)S(1)}, bf16[784,768]{1,0:T(8,128)(2,1)S(1)}, u32[]{:S(2)}, u32[]{:S(2)}) collective-permute-start(bf16[784,768]{1,0:T(8,128)(2,1)S(1)} %shard_map.154), channel_id=1, source_target_pairs={{0,2},{2,0},{1,3},{3,1},{4,6},{6,4},{5,7},{7,5},{8,10},{10,8},{9,1... | collective-permute-start | bytes 3612680 | tf_op jit(solution)/shard_map/ppermute | solution.py:625
  21.5 19.0 %collective-permute-start.1 = (bf16[144,384]{1,0:T(8,128)(2,1)S(1)}, bf16[144,384]{1,0:T(8,128)(2,1)S(1)}, u32[]{:S(2)}, u32[]{:S(2)}) collective-permute-start(bf16[144,384]{1,0:T(8,128)(2,1)S(1)} %shard_map.148.refs_2_), channel_id=1, source_target_pairs={{0,4},{4,8},{8,12},{1,5},{5,9},{9,13},{2,6},{6,10},{10,14},{3,7},{... | collective-permute-start | bytes 331784 | tf_op jit(solution)/shard_map/ppermute | solution.py:621
  25.0 15.5 %collective-permute-start.2 = (bf16[144,384]{1,0:T(8,128)(2,1)S(1)}, bf16[144,384]{1,0:T(8,128)(2,1)S(1)}, u32[]{:S(2)}, u32[]{:S(2)}) collective-permute-start(bf16[144,384]{1,0:T(8,128)(2,1)S(1)} %shard_map.148.refs_2_), channel_id=1, source_target_pairs={{0,8},{4,12},{1,9},{5,13},{2,10},{6,14},{3,11},{7,15},{16,24},{20,... | collective-permute-start | bytes 331784 | tf_op jit(solution)/shard_map/ppermute | solution.py:621
  27.3 13.2 %collective-permute-start.3 = (bf16[144,384]{1,0:T(8,128)(2,1)S(1)}, bf16[144,384]{1,0:T(8,128)(2,1)S(1)}, u32[]{:S(2)}, u32[]{:S(2)}) collective-permute-start(bf16[144,384]{1,0:T(8,128)(2,1)S(1)} %shard_map.148.refs_2_), channel_id=1, source_target_pairs={{0,12},{1,13},{2,14},{3,15},{16,28},{17,29},{18,30},{19,31}} | collective-permute-start | bytes 331784 | tf_op jit(solution)/shard_map/ppermute | solution.py:621
  40.5 3.6 %copy-start.6 = (bf16[768,768]{1,0:T(8,128)(2,1)S(1)}, bf16[768,768]{1,0:T(8,128)(2,1)}, u32[]{:S(2)}) copy-start(bf16[768,768]{1,0:T(8,128)(2,1)} %refs_9_.1) | copy-start | bytes 3538948
  40.5 3.5 %copy-start.12 = (f32[768]{0:T(1024)S(1)}, f32[768]{0:T(1024)}, u32[]{:S(2)}) copy-start(f32[768]{0:T(1024)} %refs_8_.1) | copy-start | bytes 9220
  40.6 21.3 %collective-permute-start.14 = (bf16[400,768]{1,0:T(8,128)(2,1)S(1)}, bf16[400,768]{1,0:T(8,128)(2,1)S(1)}, u32[]{:S(2)}, u32[]{:S(2)}) collective-permute-start(bf16[400,768]{1,0:T(8,128)(2,1)S(1)} %collective-permute-done.4.refs_5_.refs_6_), channel_id=1, source_target_pairs={{0,2},{2,0},{1,3},{3,1},{4,6},{6,4},{5,7},{7,5},{8,10},{10,8},{9,1... | collective-permute-start | bytes 1843208 | tf_op jit(solution)/shard_map/ppermute | solution.py:671
  41.2 24.7 %collective-permute-start.11 = (bf16[400,768]{1,0:T(8,128)(2,1)S(1)}, bf16[400,768]{1,0:T(8,128)(2,1)S(1)}, u32[]{:S(2)}, u32[]{:S(2)}) collective-permute-start(bf16[400,768]{1,0:T(8,128)(2,1)S(1)} %collective-permute-done.4.refs_5_.refs_6_), channel_id=1, source_target_pairs={{0,16},{16,0},{1,17},{17,1},{2,18},{18,2},{3,19},{19,3},{4,20},{20... | collective-permute-start | bytes 1843208 | tf_op jit(solution)/shard_map/ppermute | solution.py:672
  42.7 1.3 %collective-permute-start.5 = (bf16[128,384]{1,0:T(8,128)(2,1)S(1)}, bf16[128,384]{1,0:T(8,128)(2,1)S(1)}, u32[]{:S(2)}, u32[]{:S(2)}) collective-permute-start(bf16[128,384]{1,0:T(8,128)(2,1)S(1)} %shard_map.151.refs_5_), channel_id=1, source_target_pairs={{0,1},{1,0},{2,3},{3,2},{4,5},{5,4},{6,7},{7,6},{8,9},{9,8},{10,11... | collective-permute-start | bytes 294920 | tf_op jit(solution)/shard_map/ppermute | solution.py:673
  44.0 41.1 %copy-start.15 = (f32[768]{0:T(1024)S(1)}, f32[768]{0:T(1024)}, u32[]{:S(2)}) copy-start(f32[768]{0:T(1024)} %refs_4_.1) | copy-start | bytes 9220
  51.4 18.3 %collective-permute-start.6 = (bf16[352,768]{1,0:T(8,128)(2,1)S(1)}, bf16[352,768]{1,0:T(8,128)(2,1)S(1)}, u32[]{:S(2)}, u32[]{:S(2)}) collective-permute-start(bf16[352,768]{1,0:T(8,128)(2,1)S(1)} %get-tuple-element.40), channel_id=1, source_target_pairs={{0,4},{4,0},{8,12},{12,8},{1,5},{5,1},{9,13},{13,9},{2,6},{6,2},{1... | collective-permute-start | bytes 1622024 | tf_op jit(solution)/shard_map/ppermute | solution.py:702
  56.7 28.0 %collective-permute-start.7 = (bf16[352,768]{1,0:T(8,128)(2,1)S(1)}, bf16[352,768]{1,0:T(8,128)(2,1)S(1)}, u32[]{:S(2)}, u32[]{:S(2)}) collective-permute-start(bf16[352,768]{1,0:T(8,128)(2,1)S(1)} %get-tuple-element.41), channel_id=1, source_target_pairs={{0,2},{2,0},{1,3},{3,1},{4,6},{6,4},{5,7},{7,5},{8,10},{10,8},{9,1... | collective-permute-start | bytes 1622024 | tf_op jit(solution)/shard_map/ppermute | solution.py:703
  61.9 22.8 %collective-permute-start.8 = (bf16[352,768]{1,0:T(8,128)(2,1)S(1)}, bf16[352,768]{1,0:T(8,128)(2,1)S(1)}, u32[]{:S(2)}, u32[]{:S(2)}) collective-permute-start(bf16[352,768]{1,0:T(8,128)(2,1)S(1)} %get-tuple-element.42), channel_id=1, source_target_pairs={{0,6},{2,4},{4,2},{6,0},{8,14},{10,12},{12,10},{14,8},{1,7},{3,5},... | collective-permute-start | bytes 1622024 | tf_op jit(solution)/shard_map/ppermute | solution.py:704
  64.4 23.2 %copy-start.2 = (bf16[1,768,768]{2,1,0:T(8,128)(2,1)S(1)}, bf16[1,768,768]{2,1,0:T(8,128)(2,1)}, u32[]{:S(2)}) copy-start(bf16[1,768,768]{2,1,0:T(8,128)(2,1)} %refs_3_.5) | copy-start | bytes 3538948
  64.4 21.3 %collective-permute-start.15 = (bf16[400,768]{1,0:T(8,128)(2,1)S(1)}, bf16[400,768]{1,0:T(8,128)(2,1)S(1)}, u32[]{:S(2)}, u32[]{:S(2)}) collective-permute-start(bf16[400,768]{1,0:T(8,128)(2,1)S(1)} %collective-permute-done.14.refs_7_), channel_id=1, source_target_pairs={{0,16},{16,0},{1,17},{17,1},{2,18},{18,2},{3,19},{19,3},{4,20},{20... | collective-permute-start | bytes 1843208 | tf_op jit(solution)/shard_map/ppermute | solution.py:708
  65.9 21.6 %collective-permute-start.10 = (bf16[784,768]{1,0:T(8,128)(2,1)S(1)}, bf16[784,768]{1,0:T(8,128)(2,1)S(1)}, u32[]{:S(2)}, u32[]{:S(2)}) collective-permute-start(bf16[784,768]{1,0:T(8,128)(2,1)S(1)} %collective-permute-done.9.refs_4_), channel_id=1, source_target_pairs={{0,1},{1,0},{2,3},{3,2},{4,5},{5,4},{6,7},{7,6},{8,9},{9,8},{10,11... | collective-permute-start | bytes 3612680 | tf_op jit(solution)/shard_map/ppermute | solution.py:716
  69.7 16.1 %collective-permute-start.12 = (bf16[400,768]{1,0:T(8,128)(2,1)S(1)}, bf16[400,768]{1,0:T(8,128)(2,1)S(1)}, u32[]{:S(2)}, u32[]{:S(2)}) collective-permute-start(bf16[400,768]{1,0:T(8,128)(2,1)S(1)} %collective-permute-done.4.refs_5_.refs_6_), channel_id=1, source_target_pairs={{0,1},{1,0},{2,3},{3,2},{4,5},{5,4},{6,7},{7,6},{8,9},{9,8},{10,11... | collective-permute-start | bytes 1843208 | tf_op jit(solution)/shard_map/ppermute | solution.py:716
  84.6 5.2 %collective-permute-start.16 = (bf16[400,768]{1,0:T(8,128)(2,1)S(1)}, bf16[400,768]{1,0:T(8,128)(2,1)S(1)}, u32[]{:S(2)}, u32[]{:S(2)}) collective-permute-start(bf16[400,768]{1,0:T(8,128)(2,1)S(1)} %collective-permute-done.14.refs_7_), channel_id=1, source_target_pairs={{0,1},{1,0},{2,3},{3,2},{4,5},{5,4},{6,7},{7,6},{8,9},{9,8},{10,11... | collective-permute-start | bytes 1843208 | tf_op jit(solution)/shard_map/ppermute | solution.py:716
  84.7 2.9 %collective-permute-start.13 = (bf16[400,768]{1,0:T(8,128)(2,1)S(1)}, bf16[400,768]{1,0:T(8,128)(2,1)S(1)}, u32[]{:S(2)}, u32[]{:S(2)}) collective-permute-start(bf16[400,768]{1,0:T(8,128)(2,1)S(1)} %collective-permute-done.11.refs_7_), channel_id=1, source_target_pairs={{0,1},{1,0},{2,3},{3,2},{4,5},{5,4},{6,7},{7,6},{8,9},{9,8},{10,11... | collective-permute-start | bytes 1843208 | tf_op jit(solution)/shard_map/ppermute | solution.py:716
  85.7 4.1 %collective-permute-start.17 = (bf16[400,768]{1,0:T(8,128)(2,1)S(1)}, bf16[400,768]{1,0:T(8,128)(2,1)S(1)}, u32[]{:S(2)}, u32[]{:S(2)}) collective-permute-start(bf16[400,768]{1,0:T(8,128)(2,1)S(1)} %collective-permute-done.15.refs_8_), channel_id=1, source_target_pairs={{0,1},{1,0},{2,3},{3,2},{4,5},{5,4},{6,7},{7,6},{8,9},{9,8},{10,11... | collective-permute-start | bytes 1843208 | tf_op jit(solution)/shard_map/ppermute | solution.py:717
  96.4 8.6 %collective-permute-start.18 = (bf16[352,384]{1,0:T(8,128)(2,1)S(1)}, bf16[352,384]{1,0:T(8,128)(2,1)S(1)}, u32[]{:S(2)}, u32[]{:S(2)}) collective-permute-start(bf16[352,384]{1,0:T(8,128)(2,1)S(1)} %get-tuple-element.56), channel_id=1, source_target_pairs={{0,2},{2,0},{1,3},{3,1},{4,6},{6,4},{5,7},{7,5},{8,10},{10,8},{9,1... | collective-permute-start | bytes 811016 | tf_op jit(solution)/shard_map/ppermute | solution.py:743
  97.9 9.4 %collective-permute-start.19 = (bf16[352,384]{1,0:T(8,128)(2,1)S(1)}, bf16[352,384]{1,0:T(8,128)(2,1)S(1)}, u32[]{:S(2)}, u32[]{:S(2)}) collective-permute-start(bf16[352,384]{1,0:T(8,128)(2,1)S(1)} %get-tuple-element.57), channel_id=1, source_target_pairs={{0,4},{4,0},{8,12},{12,8},{1,5},{5,1},{9,13},{13,9},{2,6},{6,2},{1... | collective-permute-start | bytes 811016 | tf_op jit(solution)/shard_map/ppermute | solution.py:741
  99.5 12.4 %collective-permute-start.20 = (bf16[352,384]{1,0:T(8,128)(2,1)S(1)}, bf16[352,384]{1,0:T(8,128)(2,1)S(1)}, u32[]{:S(2)}, u32[]{:S(2)}) collective-permute-start(bf16[352,384]{1,0:T(8,128)(2,1)S(1)} %get-tuple-element.58), channel_id=1, source_target_pairs={{0,6},{2,4},{4,2},{6,0},{8,14},{10,12},{12,10},{14,8},{1,7},{3,5},... | collective-permute-start | bytes 811016 | tf_op jit(solution)/shard_map/ppermute | solution.py:742
  (5 other events, 9.2 us)

commit v3 on v2

--- a/solution.py
+++ b/solution.py
@@ -486,23 +486,22 @@
         far[...] = jnp.where(place == 0, high, low).astype(BF16)
 
 
-def payload_kernel(info, bias, w_up, w_down, out, sems):
-    part = (out.shape[0] - TILE) // 2
-    first = info[3] * (out.shape[1] // 2)
-    if 2 * part < out.shape[1] // 2 + part:
-        first = first + info[2] * part
-    at = pl.ds(pl.multiple_of(first, part), part)
-    copies = [
-        pltpu.make_async_copy(w.at[0, at], out.at[pl.ds(number * part, part)], sems.at[number])
-        for number, w in enumerate((w_up, w_down))
-    ]
-    for copy in copies:
-        copy.start()
-    row = iota((TILE, out.shape[1]), 0)
-    rows = jnp.zeros((TILE, out.shape[1]), F32)
+def payload_kernel(bias, w_up, w_down, own, share, sems):
+    copies = []
+    for out, shift in ((share, lax.axis_index("groups")), (own, 0)):
+        part = (out.shape[0] - TILE) // 2
+        first = lax.axis_index("sub") * (out.shape[1] // 2) + shift * part
+        at = pl.ds(pl.multiple_of(first, part), part)
+        for number, w in enumerate((w_up, w_down)):
+            target = out.at[pl.ds(number * part, part)]
+            copies.append(pltpu.make_async_copy(w.at[0, at], target, sems.at[len(copies)]))
+            copies[-1].start()
+    row = iota((TILE, own.shape[1]), 0)
+    rows = jnp.zeros((TILE, own.shape[1]), F32)
     for number, term in enumerate(split(bias[...], 3)):
         rows = jnp.where(row == number, term.astype(F32), rows)
-    out[2 * part :, :] = rows.astype(BF16)
+    for out in (own, share):
+        out[out.shape[0] - TILE :, :] = rows.astype(BF16)
     for copy in copies:
         copy.wait()
 
@@ -566,19 +565,15 @@
     side = width // 2
 
     part = width // 4
-    def payload(rows, room, after):
-        return call(
-            payload_kernel,
-            arr((2 * rows + TILE, width), BF16),
-            micros=0.001,
-            room=room,
-            in_specs=[SMEM, VMEM, ANY, ANY],
-            out_specs=VMEM,
-            scratch_shapes=[pltpu.SemaphoreType.DMA((2,))],
-            after=after,
-        )(info, b_up, w_up, w_down)
-
-    share = payload(part, 62, ())
+    half, share = call(
+        payload_kernel,
+        (arr((4 * part + TILE, width), BF16), arr((2 * part + TILE, width), BF16)),
+        micros=0.001,
+        room=62,
+        in_specs=[VMEM, ANY, ANY],
+        out_specs=(VMEM, VMEM),
+        scratch_shapes=[pltpu.SemaphoreType.DMA((4,))],
+    )(b_up, w_up, w_down)
     far = lax.ppermute(share, "tm", [(i, i ^ 2) for i in range(shard_count)])
 
     rows = 2 * SPAN
@@ -622,7 +617,7 @@
         for hop in range(1, shard_count)
     ]
 
-    own = lax.ppermute(payload(2 * part, 24, (summary,)), "mp", swap)
+    own = lax.ppermute(tie(half, summary), "mp", swap)
     slot, column, flag = call(
         lambda *refs: route_kernel(cold, *refs),
         (arr((1, length), jnp.int32), arr((length, 128), jnp.int32), arr((1,), jnp.int32)),

time: 115 us -> 113 us (0.983)
  waiting for transfers between devices: 38.5 us -> 34.5 us
  starting transfers between devices: 28.8 us -> 31.4 us
    ppermute x1, waiting for transfers between devices: 4.71 us -> 1.4 us  [fast(): far_x = lax.ppermute(far, 'mp', swap)]
    ppermute x1, waiting for transfers between devices: 14.9 us -> 12.6 us  [fast(): lax.ppermute(beside_rows, 'mp', swap)]
    ppermute x1, starting transfers between devices: 2.5 us -> 4.16 us  [fast(): lax.ppermute(other, ('tm', 'mp'), near_x)]
    ppermute x1, waiting for transfers between devices: 3.79 us -> 5.37 us  [fast(): lax.ppermute(same, 'tm', near)]
    pallas_call x13 -> x12, Pallas kernels: 44.2 us -> 44.7 us  [call(): return lambda *args: run(*args, *after)]
where the time goes in v3:
time: 113 us
  Pallas kernels  44.7 us (40%)
  waiting for transfers between devices  34.5 us (31%)
  starting transfers between devices  31.4 us (28%)
  local copies, waits for them, and re-layouts  2.25 us (2%)
    pallas_call x12, Pallas kernels, call(): return lambda *args: run(*args, *after)  44.7 us
    ppermute x1, waiting for transfers between devices, fast(): lax.ppermute(beside_rows, 'mp', swap)  12.6 us
    ppermute x3, starting transfers between devices, fast(): lax.ppermute(chip, 'tm', [(i, i + hop) for i in range(shard_count - hop)])  7.03 us
    ppermute x1, waiting for transfers between devices, fast(): lax.ppermute(same, 'tm', near)  5.37 us
    ppermute x1, starting transfers between devices, fast(): lax.ppermute(same, 'tm', near)  5.1 us
    ppermute x1, waiting for transfers between devices, fast(): back_l = lax.ppermute(other_l, 'mp', swap)  5.03 us
    ppermute x1, waiting for transfers between devices, fast(): back_other = lax.ppermute(other, ('tm', 'mp'), near_x)  4.95 us
    ppermute x1, starting transfers between devices, fast(): lax.ppermute(other, ('tm', 'mp'), near_x)  4.16 us
  transfers between devices with their start and end apart: 21, of which 8 were waited for; matrix products, arithmetic and copies ran while one was open for 0% of the time, Pallas kernels for 28%

profile of v3, /device:TPU:0, one launch (start us, length us, event | category | flops | bytes accessed | tf_op | source)
XLA Modules:
  0.0 113.1 jit_solution(8147775061004287210)
XLA Ops:
  0.0 3.4 %shard_map.146 = (bf16[784,768]{1,0:T(8,128)(2,1)}, bf16[400,768]{1,0:T(8,128)(2,1)}) custom-call(f32[1,768]{1,0:T(1,128)} %refs_1_.9, bf16[1,768,768]{2,1,0:T(8,128)(2,1)} %refs_2_.7, bf16[1,768,768]{2,1,0:T(8,128)(2,1)} %refs_3_.1), custom_call_target="tpu_custom_call" | custom-call | flops 1000000 | bytes 3000 | tf_op jit(solution)/shard_map/pallas_call | solution.py:184
  3.4 4.1 %collective-permute-start.4 = (bf16[400,768]{1,0:T(8,128)(2,1)}, bf16[400,768]{1,0:T(8,128)(2,1)}, u32[]{:S(2)}, u32[]{:S(2)}) collective-permute-start(bf16[400,768]{1,0:T(8,128)(2,1)} %get-tuple-element.37.refs_6_), channel_id=1, source_target_pairs={{0,8},{4,12},{8,0},{12,4},{1,9},{5,13},{9,1},{13,5},{2,10},{6,14},... | collective-permute-start | bytes 1843208 | tf_op jit(solution)/shard_map/ppermute | solution.py:577
  7.5 8.9 %shard_map.147 = (bf16[1024,768]{1,0:T(8,128)(2,1)}, bf16[1024,256]{1,0:T(8,128)(2,1)}, bf16[144,768]{1,0:T(8,128)(2,1)}) custom-call(bf16[1024,768]{1,0:T(8,128)(2,1)} %refs_0_.5, bf16[768,768]{1,0:T(8,128)(2,1)} %refs_1_.7, bf16[768,256]{1,0:T(8,128)(2,1)} %refs_2_.5, bf16[12,768]{1,0:T(8,128)(2,1)} %bitcast.8, f32[1,12]{1,0:T(1,128)} %bitcast.9, ...), custom_call_target="tpu_custom_call" | custom-call | flops 1000000 | bytes 3000 | tf_op jit(solution)/shard_map/pallas_call | solution.py:184
  16.5 1.6 %collective-permute-start.9 = (bf16[784,768]{1,0:T(8,128)(2,1)}, bf16[784,768]{1,0:T(8,128)(2,1)S(1)}, u32[]{:S(2)}, u32[]{:S(2)}) collective-permute-start(bf16[784,768]{1,0:T(8,128)(2,1)} %get-tuple-element.51), channel_id=1, source_target_pairs={{0,2},{2,0},{1,3},{3,1},{4,6},{6,4},{5,7},{7,5},{8,10},{10,8},{9,1... | collective-permute-start | bytes 3612680 | tf_op jit(solution)/shard_map/ppermute | solution.py:620
  18.2 0.9 copy-done.8
  19.1 0.6 shard_map.148.refs_2_
  19.7 3.5 %collective-permute-start.1 = (bf16[144,384]{1,0:T(8,128)(2,1)S(1)}, bf16[144,384]{1,0:T(8,128)(2,1)S(1)}, u32[]{:S(2)}, u32[]{:S(2)}) collective-permute-start(bf16[144,384]{1,0:T(8,128)(2,1)S(1)} %shard_map.148.refs_2_), channel_id=1, source_target_pairs={{0,4},{4,8},{8,12},{1,5},{5,9},{9,13},{2,6},{6,10},{10,14},{3,7},{... | collective-permute-start | bytes 331784 | tf_op jit(solution)/shard_map/ppermute | solution.py:616
  23.2 2.2 %collective-permute-start.2 = (bf16[144,384]{1,0:T(8,128)(2,1)S(1)}, bf16[144,384]{1,0:T(8,128)(2,1)S(1)}, u32[]{:S(2)}, u32[]{:S(2)}) collective-permute-start(bf16[144,384]{1,0:T(8,128)(2,1)S(1)} %shard_map.148.refs_2_), channel_id=1, source_target_pairs={{0,8},{4,12},{1,9},{5,13},{2,10},{6,14},{3,11},{7,15},{16,24},{20,... | collective-permute-start | bytes 331784 | tf_op jit(solution)/shard_map/ppermute | solution.py:616
  25.5 1.3 %collective-permute-start.3 = (bf16[144,384]{1,0:T(8,128)(2,1)S(1)}, bf16[144,384]{1,0:T(8,128)(2,1)S(1)}, u32[]{:S(2)}, u32[]{:S(2)}) collective-permute-start(bf16[144,384]{1,0:T(8,128)(2,1)S(1)} %shard_map.148.refs_2_), channel_id=1, source_target_pairs={{0,12},{1,13},{2,14},{3,15},{16,28},{17,29},{18,30},{19,31}} | collective-permute-start | bytes 331784 | tf_op jit(solution)/shard_map/ppermute | solution.py:616
  26.8 1.7 %shard_map.145 = (s32[1,1024]{1,0:T(1,128)S(1)}, s32[1024,128]{1,0:T(8,128)S(1)}, s32[1]{0:T(128)}) custom-call(s32[4]{0:T(128)S(1)} %pad_add_fusion.refs_0_, s32[16]{0:T(128)S(1)} %copy-done.12, s32[1,1024]{1,0:T(1,128)S(1)} %bitcast.7), custom_call_target="tpu_custom_call" | custom-call | flops 1000000 | bytes 3000 | tf_op jit(solution)/shard_map/pallas_call | solution.py:184
  28.5 1.3 %copy-done.6 = bf16[768,768]{1,0:T(8,128)(2,1)S(1)} copy-done((bf16[768,768]{1,0:T(8,128)(2,1)S(1)}, bf16[768,768]{1,0:T(8,128)(2,1)}, u32[]{:S(2)}) %copy-start.6) | copy-done | bytes 1179672
  29.8 2.3 %shard_map.149.refs_3_.refs_2_ = f32[1024,768]{1,0:T(8,128)S(1)} custom-call(bf16[1024,768]{1,0:T(8,128)(2,1)S(1)} %copy-done, bf16[768,768]{1,0:T(8,128)(2,1)S(1)} %copy-done.6, bf16[144,384]{1,0:T(8,128)(2,1)S(1)} %shard_map.148.refs_2_, s32[1,1024]{1,0:T(1,128)S(1)} %get-tuple-element.41.refs_3_.refs_4_.refs_10_), custom_call_target="tpu_custom_call" | custom-call | flops 1000000 | bytes 3000 | tf_op jit(solution)/shard_map/pallas_call | solution.py:184
  32.1 7.8 %shard_map.150 = (f32[1024,768]{1,0:T(8,128)S(1)}, f32[1024,12]{1,0:T(8,128)S(1)}) custom-call(bf16[1024,768]{1,0:T(8,128)(2,1)S(1)} %copy-done.4, bf16[1024,256]{1,0:T(8,128)(2,1)S(1)} %copy-done.3, f32[12,1024]{1,0:T(8,128)S(1)} %copy-done.7, f32[1024,768]{1,0:T(8,128)S(1)} %shard_map.149.refs_3_.refs_2_), custom_call_target="tpu_custom_call" | custom-call | flops 1000000 | bytes 3000 | tf_op jit(solution)/shard_map/pallas_call | solution.py:184
  40.0 1.5 %collective-permute-start.14 = (bf16[400,768]{1,0:T(8,128)(2,1)}, bf16[400,768]{1,0:T(8,128)(2,1)S(1)}, u32[]{:S(2)}, u32[]{:S(2)}) collective-permute-start(bf16[400,768]{1,0:T(8,128)(2,1)} %collective-permute-done.4.refs_5_.refs_6_), channel_id=1, source_target_pairs={{0,2},{2,0},{1,3},{3,1},{4,6},{6,4},{5,7},{7,5},{8,10},{10,8},{9,1... | collective-permute-start | bytes 1843208 | tf_op jit(solution)/shard_map/ppermute | solution.py:666
  41.5 1.5 %collective-permute-start.11 = (bf16[400,768]{1,0:T(8,128)(2,1)}, bf16[400,768]{1,0:T(8,128)(2,1)S(1)}, u32[]{:S(2)}, u32[]{:S(2)}) collective-permute-start(bf16[400,768]{1,0:T(8,128)(2,1)} %collective-permute-done.4.refs_5_.refs_6_), channel_id=1, source_target_pairs={{0,16},{16,0},{1,17},{17,1},{2,18},{18,2},{3,19},{19,3},{4,20},{20... | collective-permute-start | bytes 1843208 | tf_op jit(solution)/shard_map/ppermute | solution.py:667
  43.1 1.3 %collective-permute-done.5.refs_6_ = bf16[128,384]{1,0:T(8,128)(2,1)S(1)} collective-permute-done((bf16[128,384]{1,0:T(8,128)(2,1)S(1)}, bf16[128,384]{1,0:T(8,128)(2,1)S(1)}, u32[]{:S(2)}, u32[]{:S(2)}) %collective-permute-start.5) | collective-permute-done | bytes 98336 | tf_op jit(solution)/shard_map/ppermute | solution.py:668
  44.4 7.4 %shard_map.152 = (bf16[352,768]{1,0:T(8,128)(2,1)S(1)}, bf16[352,768]{1,0:T(8,128)(2,1)S(1)}, bf16[352,768]{1,0:T(8,128)(2,1)S(1)}, bf16[352,768]{1,0:T(8,128)(2,1)S(1)}) custom-call(s32[4]{0:T(128)S(1)} %pad_add_fusion.refs_0_, f32[1024,768]{1,0:T(8,128)S(1)} %get-tuple-element.42.refs_1_, f32[1024,768]{1,0:T(8,128)S(1)} %shard_map.149.refs_3_.refs_2_, ...), custom_call_target="tpu_custom_call" | custom-call | flops 1000000 | bytes 3000 | tf_op jit(solution)/shard_map/pallas_call | solution.py:184
  51.8 5.1 %collective-permute-start.6 = (bf16[352,768]{1,0:T(8,128)(2,1)S(1)}, bf16[352,768]{1,0:T(8,128)(2,1)S(1)}, u32[]{:S(2)}, u32[]{:S(2)}) collective-permute-start(bf16[352,768]{1,0:T(8,128)(2,1)S(1)} %get-tuple-element.44), channel_id=1, source_target_pairs={{0,4},{4,0},{8,12},{12,8},{1,5},{5,1},{9,13},{13,9},{2,6},{6,2},{1... | collective-permute-start | bytes 1622024 | tf_op jit(solution)/shard_map/ppermute | solution.py:697
  57.4 1.4 %collective-permute-done.14.refs_7_ = bf16[400,768]{1,0:T(8,128)(2,1)S(1)} collective-permute-done((bf16[400,768]{1,0:T(8,128)(2,1)}, bf16[400,768]{1,0:T(8,128)(2,1)S(1)}, u32[]{:S(2)}, u32[]{:S(2)}) %collective-permute-start.14) | collective-permute-done | bytes 614432 | tf_op jit(solution)/shard_map/ppermute | solution.py:666
  58.8 4.2 %collective-permute-start.8 = (bf16[352,768]{1,0:T(8,128)(2,1)S(1)}, bf16[352,768]{1,0:T(8,128)(2,1)S(1)}, u32[]{:S(2)}, u32[]{:S(2)}) collective-permute-start(bf16[352,768]{1,0:T(8,128)(2,1)S(1)} %get-tuple-element.46), channel_id=1, source_target_pairs={{0,6},{2,4},{4,2},{6,0},{8,14},{10,12},{12,10},{14,8},{1,7},{3,5},... | collective-permute-start | bytes 1622024 | tf_op jit(solution)/shard_map/ppermute | solution.py:699
  63.0 1.6 %collective-permute-start.15 = (bf16[400,768]{1,0:T(8,128)(2,1)S(1)}, bf16[400,768]{1,0:T(8,128)(2,1)S(1)}, u32[]{:S(2)}, u32[]{:S(2)}) collective-permute-start(bf16[400,768]{1,0:T(8,128)(2,1)S(1)} %collective-permute-done.14.refs_7_), channel_id=1, source_target_pairs={{0,16},{16,0},{1,17},{17,1},{2,18},{18,2},{3,19},{19,3},{4,20},{20... | collective-permute-start | bytes 1843208 | tf_op jit(solution)/shard_map/ppermute | solution.py:703
  64.6 5.4 %collective-permute-done.6.refs_0_ = bf16[352,768]{1,0:T(8,128)(2,1)S(1)} collective-permute-done((bf16[352,768]{1,0:T(8,128)(2,1)S(1)}, bf16[352,768]{1,0:T(8,128)(2,1)S(1)}, u32[]{:S(2)}, u32[]{:S(2)}) %collective-permute-start.6) | collective-permute-done | bytes 540704 | tf_op jit(solution)/shard_map/ppermute | solution.py:697
  69.9 12.6 %collective-permute-done.7.refs_1_ = bf16[352,768]{1,0:T(8,128)(2,1)S(1)} collective-permute-done((bf16[352,768]{1,0:T(8,128)(2,1)S(1)}, bf16[352,768]{1,0:T(8,128)(2,1)S(1)}, u32[]{:S(2)}, u32[]{:S(2)}) %collective-permute-start.7) | collective-permute-done | bytes 540704 | tf_op jit(solution)/shard_map/ppermute | solution.py:698
  83.7 1.7 %collective-permute-done.13.refs_9_ = bf16[400,768]{1,0:T(8,128)(2,1)S(1)} collective-permute-done((bf16[400,768]{1,0:T(8,128)(2,1)S(1)}, bf16[400,768]{1,0:T(8,128)(2,1)S(1)}, u32[]{:S(2)}, u32[]{:S(2)}) %collective-permute-start.13) | collective-permute-done | bytes 614432 | tf_op jit(solution)/shard_map/ppermute | solution.py:711
  85.4 2.9 %shard_map.154 = (bf16[3,768,768]{2,1,0:T(8,128)(2,1)S(1)}, bf16[3,768,768]{2,1,0:T(8,128)(2,1)S(1)}, f32[4,768]{1,0:T(4,128)S(1)}) custom-call(s32[4]{0:T(128)S(1)} %pad_add_fusion.refs_0_, f32[1,768]{1,0:T(1,128)S(1)} %copy-done.9, bf16[1,768,768]{2,1,0:T(8,128)(2,1)S(1)} %copy-done.1, bf16[1,768,768]{2,1,0:T(8,128)(2,1)S(1)} %copy-done.2, ...), custom_call_target="tpu_custom_call" | custom-call | flops 100000000 | bytes 300000 | tf_op jit(solution)/shard_map/pallas_call | solution.py:184
  88.3 6.5 %shard_map.155 = (bf16[352,384]{1,0:T(8,128)(2,1)S(1)}, bf16[352,384]{1,0:T(8,128)(2,1)S(1)}, bf16[352,384]{1,0:T(8,128)(2,1)S(1)}, bf16[352,384]{1,0:T(8,128)(2,1)S(1)}) custom-call(s32[4]{0:T(128)S(1)} %pad_add_fusion.refs_0_, s32[1]{0:T(128)} %get-tuple-element.36.refs_1_, bf16[352,768]{1,0:T(8,128)(2,1)S(1)} %get-tuple-element.48.refs_2_, ...), custom_call_target="tpu_custom_call" | custom-call | flops 8999999488 | bytes 27000000 | tf_op jit(solution)/shard_map/pallas_call | solution.py:184
  94.8 1.0 collective-permute-start.18
  95.9 2.3 %collective-permute-start.19 = (bf16[352,384]{1,0:T(8,128)(2,1)S(1)}, bf16[352,384]{1,0:T(8,128)(2,1)S(1)}, u32[]{:S(2)}, u32[]{:S(2)}) collective-permute-start(bf16[352,384]{1,0:T(8,128)(2,1)S(1)} %get-tuple-element.63), channel_id=1, source_target_pairs={{0,4},{4,0},{8,12},{12,8},{1,5},{5,1},{9,13},{13,9},{2,6},{6,2},{1... | collective-permute-start | bytes 811016 | tf_op jit(solution)/shard_map/ppermute | solution.py:736
  98.4 5.0 %collective-permute-done.18.refs_2_ = bf16[352,384]{1,0:T(8,128)(2,1)S(1)} collective-permute-done((bf16[352,384]{1,0:T(8,128)(2,1)S(1)}, bf16[352,384]{1,0:T(8,128)(2,1)S(1)}, u32[]{:S(2)}, u32[]{:S(2)}) %collective-permute-start.18) | collective-permute-done | bytes 270368 | tf_op jit(solution)/shard_map/ppermute | solution.py:738
  103.4 2.1 %collective-permute-done.19.refs_3_ = bf16[352,384]{1,0:T(8,128)(2,1)S(1)} collective-permute-done((bf16[352,384]{1,0:T(8,128)(2,1)S(1)}, bf16[352,384]{1,0:T(8,128)(2,1)S(1)}, u32[]{:S(2)}, u32[]{:S(2)}) %collective-permute-start.19) | collective-permute-done | bytes 270368 | tf_op jit(solution)/shard_map/ppermute | solution.py:736
  105.5 5.0 %collective-permute-done.20.refs_4_ = bf16[352,384]{1,0:T(8,128)(2,1)S(1)} collective-permute-done((bf16[352,384]{1,0:T(8,128)(2,1)S(1)}, bf16[352,384]{1,0:T(8,128)(2,1)S(1)}, u32[]{:S(2)}, u32[]{:S(2)}) %collective-permute-start.20) | collective-permute-done | bytes 270368 | tf_op jit(solution)/shard_map/ppermute | solution.py:737
  110.4 2.7 %shard_map.156 = bf16[1024,384]{1,0:T(8,128)(2,1)} custom-call(s32[1024,128]{1,0:T(8,128)S(1)} %get-tuple-element.35.refs_0_, bf16[352,384]{1,0:T(8,128)(2,1)S(1)} %get-tuple-element.61.refs_1_, bf16[352,384]{1,0:T(8,128)(2,1)S(1)} %collective-permute-done.18.refs_2_, bf16[352,384]{1,0:T(8,128)(2,1)S(1)} %collective-permute-done.19.refs_3_, ...), custom_call_target="tpu_custom_call" | custom-call | flops 1000000000 | bytes 3000000 | tf_op jit(solution)/shard_map/pallas_call | solution.py:184
  (51 shorter events, 2.2 us)
Async XLA Ops:
  3.4 36.5 %collective-permute-start.4 = (bf16[400,768]{1,0:T(8,128)(2,1)}, bf16[400,768]{1,0:T(8,128)(2,1)}, u32[]{:S(2)}, u32[]{:S(2)}) collective-permute-start(bf16[400,768]{1,0:T(8,128)(2,1)} %get-tuple-element.37.refs_6_), channel_id=1, source_target_pairs={{0,8},{4,12},{8,0},{12,4},{1,9},{5,13},{9,1},{13,5},{2,10},{6,14},... | collective-permute-start | bytes 1843208 | tf_op jit(solution)/shard_map/ppermute | solution.py:577
  7.5 19.3 %copy-start.11 = (s32[1024]{0:T(1024)S(1)}, s32[1024]{0:T(1024)}, u32[]{:S(2)}) copy-start(s32[1024]{0:T(1024)} %param.25) | copy-start | bytes 12292
  7.5 19.3 %copy-start.12 = (s32[16]{0:T(128)S(1)}, s32[16]{0:T(128)}, u32[]{:S(2)}) copy-start(s32[16]{0:T(128)} %refs_1_.5) | copy-start | bytes 196
  7.5 21.0 %copy-start = (bf16[1024,768]{1,0:T(8,128)(2,1)S(1)}, bf16[1024,768]{1,0:T(8,128)(2,1)}, u32[]{:S(2)}) copy-start(bf16[1024,768]{1,0:T(8,128)(2,1)} %refs_0_.5) | copy-start | bytes 4718596
  16.4 1.8 %collective-permute-start = (bf16[144,768]{1,0:T(8,128)(2,1)}, bf16[144,768]{1,0:T(8,128)(2,1)S(1)}, u32[]{:S(2)}, u32[]{:S(2)}) collective-permute-start(bf16[144,768]{1,0:T(8,128)(2,1)} %get-tuple-element.40.refs_1_), channel_id=1, source_target_pairs={{0,1},{1,0},{2,3},{3,2},{4,5},{5,4},{6,7},{7,6},{8,9},{9,8},{10,11... | collective-permute-start | bytes 663560 | tf_op jit(solution)/shard_map/ppermute | solution.py:607
  16.5 46.5 %collective-permute-start.9 = (bf16[784,768]{1,0:T(8,128)(2,1)}, bf16[784,768]{1,0:T(8,128)(2,1)S(1)}, u32[]{:S(2)}, u32[]{:S(2)}) collective-permute-start(bf16[784,768]{1,0:T(8,128)(2,1)} %get-tuple-element.51), channel_id=1, source_target_pairs={{0,2},{2,0},{1,3},{3,1},{4,6},{6,4},{5,7},{7,5},{8,10},{10,8},{9,1... | collective-permute-start | bytes 3612680 | tf_op jit(solution)/shard_map/ppermute | solution.py:620
  19.7 20.2 %collective-permute-start.1 = (bf16[144,384]{1,0:T(8,128)(2,1)S(1)}, bf16[144,384]{1,0:T(8,128)(2,1)S(1)}, u32[]{:S(2)}, u32[]{:S(2)}) collective-permute-start(bf16[144,384]{1,0:T(8,128)(2,1)S(1)} %shard_map.148.refs_2_), channel_id=1, source_target_pairs={{0,4},{4,8},{8,12},{1,5},{5,9},{9,13},{2,6},{6,10},{10,14},{3,7},{... | collective-permute-start | bytes 331784 | tf_op jit(solution)/shard_map/ppermute | solution.py:616
  23.2 16.7 %collective-permute-start.2 = (bf16[144,384]{1,0:T(8,128)(2,1)S(1)}, bf16[144,384]{1,0:T(8,128)(2,1)S(1)}, u32[]{:S(2)}, u32[]{:S(2)}) collective-permute-start(bf16[144,384]{1,0:T(8,128)(2,1)S(1)} %shard_map.148.refs_2_), channel_id=1, source_target_pairs={{0,8},{4,12},{1,9},{5,13},{2,10},{6,14},{3,11},{7,15},{16,24},{20,... | collective-permute-start | bytes 331784 | tf_op jit(solution)/shard_map/ppermute | solution.py:616
  25.5 14.4 %collective-permute-start.3 = (bf16[144,384]{1,0:T(8,128)(2,1)S(1)}, bf16[144,384]{1,0:T(8,128)(2,1)S(1)}, u32[]{:S(2)}, u32[]{:S(2)}) collective-permute-start(bf16[144,384]{1,0:T(8,128)(2,1)S(1)} %shard_map.148.refs_2_), channel_id=1, source_target_pairs={{0,12},{1,13},{2,14},{3,15},{16,28},{17,29},{18,30},{19,31}} | collective-permute-start | bytes 331784 | tf_op jit(solution)/shard_map/ppermute | solution.py:616
  29.8 2.3 %copy-start.4 = (bf16[1024,768]{1,0:T(8,128)(2,1)S(1)}, bf16[1024,768]{1,0:T(8,128)(2,1)}, u32[]{:S(2)}) copy-start(bf16[1024,768]{1,0:T(8,128)(2,1)} %get-tuple-element.38.refs_0_) | copy-start | bytes 4718596
  29.8 2.3 %copy-start.7 = (f32[12,1024]{1,0:T(8,128)S(1)}, f32[12,1024]{1,0:T(8,128)}, u32[]{:S(2)}) copy-start(f32[12,1024]{1,0:T(8,128)} %refs_2_.6) | copy-start | bytes 147460
  39.9 4.5 %copy-start.5 = (bf16[768,768]{1,0:T(8,128)(2,1)S(1)}, bf16[768,768]{1,0:T(8,128)(2,1)}, u32[]{:S(2)}) copy-start(bf16[768,768]{1,0:T(8,128)(2,1)} %refs_9_.1) | copy-start | bytes 3538948
  39.9 4.5 %copy-start.10 = (f32[768]{0:T(1024)S(1)}, f32[768]{0:T(1024)}, u32[]{:S(2)}) copy-start(f32[768]{0:T(1024)} %refs_8_.1) | copy-start | bytes 9220
  40.0 18.8 %collective-permute-start.14 = (bf16[400,768]{1,0:T(8,128)(2,1)}, bf16[400,768]{1,0:T(8,128)(2,1)S(1)}, u32[]{:S(2)}, u32[]{:S(2)}) collective-permute-start(bf16[400,768]{1,0:T(8,128)(2,1)} %collective-permute-done.4.refs_5_.refs_6_), channel_id=1, source_target_pairs={{0,2},{2,0},{1,3},{3,1},{4,6},{6,4},{5,7},{7,5},{8,10},{10,8},{9,1... | collective-permute-start | bytes 1843208 | tf_op jit(solution)/shard_map/ppermute | solution.py:666
  41.5 23.0 %collective-permute-start.11 = (bf16[400,768]{1,0:T(8,128)(2,1)}, bf16[400,768]{1,0:T(8,128)(2,1)S(1)}, u32[]{:S(2)}, u32[]{:S(2)}) collective-permute-start(bf16[400,768]{1,0:T(8,128)(2,1)} %collective-permute-done.4.refs_5_.refs_6_), channel_id=1, source_target_pairs={{0,16},{16,0},{1,17},{17,1},{2,18},{18,2},{3,19},{19,3},{4,20},{20... | collective-permute-start | bytes 1843208 | tf_op jit(solution)/shard_map/ppermute | solution.py:667
  43.1 1.3 %collective-permute-start.5 = (bf16[128,384]{1,0:T(8,128)(2,1)S(1)}, bf16[128,384]{1,0:T(8,128)(2,1)S(1)}, u32[]{:S(2)}, u32[]{:S(2)}) collective-permute-start(bf16[128,384]{1,0:T(8,128)(2,1)S(1)} %shard_map.151.refs_5_), channel_id=1, source_target_pairs={{0,1},{1,0},{2,3},{3,2},{4,5},{5,4},{6,7},{7,6},{8,9},{9,8},{10,11... | collective-permute-start | bytes 294920 | tf_op jit(solution)/shard_map/ppermute | solution.py:668
  44.4 38.6 %copy-start.13 = (f32[768]{0:T(1024)S(1)}, f32[768]{0:T(1024)}, u32[]{:S(2)}) copy-start(f32[768]{0:T(1024)} %refs_4_.1) | copy-start | bytes 9220
  51.8 18.2 %collective-permute-start.6 = (bf16[352,768]{1,0:T(8,128)(2,1)S(1)}, bf16[352,768]{1,0:T(8,128)(2,1)S(1)}, u32[]{:S(2)}, u32[]{:S(2)}) collective-permute-start(bf16[352,768]{1,0:T(8,128)(2,1)S(1)} %get-tuple-element.44), channel_id=1, source_target_pairs={{0,4},{4,0},{8,12},{12,8},{1,5},{5,1},{9,13},{13,9},{2,6},{6,2},{1... | collective-permute-start | bytes 1622024 | tf_op jit(solution)/shard_map/ppermute | solution.py:697
  56.9 25.6 %collective-permute-start.7 = (bf16[352,768]{1,0:T(8,128)(2,1)S(1)}, bf16[352,768]{1,0:T(8,128)(2,1)S(1)}, u32[]{:S(2)}, u32[]{:S(2)}) collective-permute-start(bf16[352,768]{1,0:T(8,128)(2,1)S(1)} %get-tuple-element.45), channel_id=1, source_target_pairs={{0,2},{2,0},{1,3},{3,1},{4,6},{6,4},{5,7},{7,5},{8,10},{10,8},{9,1... | collective-permute-start | bytes 1622024 | tf_op jit(solution)/shard_map/ppermute | solution.py:698
  58.8 23.7 %collective-permute-start.8 = (bf16[352,768]{1,0:T(8,128)(2,1)S(1)}, bf16[352,768]{1,0:T(8,128)(2,1)S(1)}, u32[]{:S(2)}, u32[]{:S(2)}) collective-permute-start(bf16[352,768]{1,0:T(8,128)(2,1)S(1)} %get-tuple-element.46), channel_id=1, source_target_pairs={{0,6},{2,4},{4,2},{6,0},{8,14},{10,12},{12,10},{14,8},{1,7},{3,5},... | collective-permute-start | bytes 1622024 | tf_op jit(solution)/shard_map/ppermute | solution.py:699
  62.9 22.5 %copy-start.1 = (bf16[1,768,768]{2,1,0:T(8,128)(2,1)S(1)}, bf16[1,768,768]{2,1,0:T(8,128)(2,1)}, u32[]{:S(2)}) copy-start(bf16[1,768,768]{2,1,0:T(8,128)(2,1)} %refs_2_.7) | copy-start | bytes 3538948
  63.0 22.5 %copy-start.2 = (bf16[1,768,768]{2,1,0:T(8,128)(2,1)S(1)}, bf16[1,768,768]{2,1,0:T(8,128)(2,1)}, u32[]{:S(2)}) copy-start(bf16[1,768,768]{2,1,0:T(8,128)(2,1)} %refs_3_.1) | copy-start | bytes 3538948
  63.0 22.5 %copy-start.9 = (f32[1,768]{1,0:T(1,128)S(1)}, f32[1,768]{1,0:T(1,128)}, u32[]{:S(2)}) copy-start(f32[1,768]{1,0:T(1,128)} %refs_1_.9) | copy-start | bytes 9220
  63.0 20.6 %collective-permute-start.15 = (bf16[400,768]{1,0:T(8,128)(2,1)S(1)}, bf16[400,768]{1,0:T(8,128)(2,1)S(1)}, u32[]{:S(2)}, u32[]{:S(2)}) collective-permute-start(bf16[400,768]{1,0:T(8,128)(2,1)S(1)} %collective-permute-done.14.refs_7_), channel_id=1, source_target_pairs={{0,16},{16,0},{1,17},{17,1},{2,18},{18,2},{3,19},{19,3},{4,20},{20... | collective-permute-start | bytes 1843208 | tf_op jit(solution)/shard_map/ppermute | solution.py:703
  64.5 20.9 %collective-permute-start.10 = (bf16[784,768]{1,0:T(8,128)(2,1)S(1)}, bf16[784,768]{1,0:T(8,128)(2,1)S(1)}, u32[]{:S(2)}, u32[]{:S(2)}) collective-permute-start(bf16[784,768]{1,0:T(8,128)(2,1)S(1)} %collective-permute-done.9.refs_4_), channel_id=1, source_target_pairs={{0,1},{1,0},{2,3},{3,2},{4,5},{5,4},{6,7},{7,6},{8,9},{9,8},{10,11... | collective-permute-start | bytes 3612680 | tf_op jit(solution)/shard_map/ppermute | solution.py:711
  69.9 13.7 %collective-permute-start.12 = (bf16[400,768]{1,0:T(8,128)(2,1)}, bf16[400,768]{1,0:T(8,128)(2,1)S(1)}, u32[]{:S(2)}, u32[]{:S(2)}) collective-permute-start(bf16[400,768]{1,0:T(8,128)(2,1)} %collective-permute-done.4.refs_5_.refs_6_), channel_id=1, source_target_pairs={{0,1},{1,0},{2,3},{3,2},{4,5},{5,4},{6,7},{7,6},{8,9},{9,8},{10,11... | collective-permute-start | bytes 1843208 | tf_op jit(solution)/shard_map/ppermute | solution.py:711
  82.5 5.8 %collective-permute-start.16 = (bf16[400,768]{1,0:T(8,128)(2,1)S(1)}, bf16[400,768]{1,0:T(8,128)(2,1)S(1)}, u32[]{:S(2)}, u32[]{:S(2)}) collective-permute-start(bf16[400,768]{1,0:T(8,128)(2,1)S(1)} %collective-permute-done.14.refs_7_), channel_id=1, source_target_pairs={{0,1},{1,0},{2,3},{3,2},{4,5},{5,4},{6,7},{7,6},{8,9},{9,8},{10,11... | collective-permute-start | bytes 1843208 | tf_op jit(solution)/shard_map/ppermute | solution.py:711
  82.5 2.9 %collective-permute-start.13 = (bf16[400,768]{1,0:T(8,128)(2,1)S(1)}, bf16[400,768]{1,0:T(8,128)(2,1)S(1)}, u32[]{:S(2)}, u32[]{:S(2)}) collective-permute-start(bf16[400,768]{1,0:T(8,128)(2,1)S(1)} %collective-permute-done.11.refs_7_), channel_id=1, source_target_pairs={{0,1},{1,0},{2,3},{3,2},{4,5},{5,4},{6,7},{7,6},{8,9},{9,8},{10,11... | collective-permute-start | bytes 1843208 | tf_op jit(solution)/shard_map/ppermute | solution.py:711
  83.6 4.8 %collective-permute-start.17 = (bf16[400,768]{1,0:T(8,128)(2,1)S(1)}, bf16[400,768]{1,0:T(8,128)(2,1)S(1)}, u32[]{:S(2)}, u32[]{:S(2)}) collective-permute-start(bf16[400,768]{1,0:T(8,128)(2,1)S(1)} %collective-permute-done.15.refs_8_), channel_id=1, source_target_pairs={{0,1},{1,0},{2,3},{3,2},{4,5},{5,4},{6,7},{7,6},{8,9},{9,8},{10,11... | collective-permute-start | bytes 1843208 | tf_op jit(solution)/shard_map/ppermute | solution.py:712
  94.8 8.6 %collective-permute-start.18 = (bf16[352,384]{1,0:T(8,128)(2,1)S(1)}, bf16[352,384]{1,0:T(8,128)(2,1)S(1)}, u32[]{:S(2)}, u32[]{:S(2)}) collective-permute-start(bf16[352,384]{1,0:T(8,128)(2,1)S(1)} %get-tuple-element.62), channel_id=1, source_target_pairs={{0,2},{2,0},{1,3},{3,1},{4,6},{6,4},{5,7},{7,5},{8,10},{10,8},{9,1... | collective-permute-start | bytes 811016 | tf_op jit(solution)/shard_map/ppermute | solution.py:738
  95.9 9.6 %collective-permute-start.19 = (bf16[352,384]{1,0:T(8,128)(2,1)S(1)}, bf16[352,384]{1,0:T(8,128)(2,1)S(1)}, u32[]{:S(2)}, u32[]{:S(2)}) collective-permute-start(bf16[352,384]{1,0:T(8,128)(2,1)S(1)} %get-tuple-element.63), channel_id=1, source_target_pairs={{0,4},{4,0},{8,12},{12,8},{1,5},{5,1},{9,13},{13,9},{2,6},{6,2},{1... | collective-permute-start | bytes 811016 | tf_op jit(solution)/shard_map/ppermute | solution.py:736
  98.2 12.3 %collective-permute-start.20 = (bf16[352,384]{1,0:T(8,128)(2,1)S(1)}, bf16[352,384]{1,0:T(8,128)(2,1)S(1)}, u32[]{:S(2)}, u32[]{:S(2)}) collective-permute-start(bf16[352,384]{1,0:T(8,128)(2,1)S(1)} %get-tuple-element.64), channel_id=1, source_target_pairs={{0,6},{2,4},{4,2},{6,0},{8,14},{10,12},{12,10},{14,8},{1,7},{3,5},... | collective-permute-start | bytes 811016 | tf_op jit(solution)/shard_map/ppermute | solution.py:737
  (3 other events, 4.5 us)
